TPU v7x, 256 devices: a whole 4x4x8 slice. The times are simulated.
256 devices in a mesh: row: 32 (over x, z_hi, core), col: 8 (over y, z_lo).
Axes of the slice: x: 4, y: 4, z: 8 (z_hi: 4, z_lo: 2; z = z_hi * 2 + z_lo), core: 2. Of those that a mesh axis runs over, the one named last changes fastest.
Arguments:
- activations: bfloat16 [1024, 18432], P('row', 'col'), may hold values from -6 to 6
- out_grads: bfloat16 [1024, 7168], P('col', 'row'), may hold values from -1 to 1
- query_acts: bfloat16 [64, 18432], P('row', 'col'), may hold values from -6 to 6
- query_grads: bfloat16 [64, 7168], P('col', 'row'), may hold values from -1 to 1
- basis_in: bfloat16 [18432, 18432], P('col', 'row'), may hold values from -0.046875 to 0.046875
- basis_out: bfloat16 [7168, 7168], P('row', 'col'), may hold values from -0.0625 to 0.0625
- damping: float32 [1], replicated, may hold values from 0.1 to 1
Outputs:
- corrected: float32 [7168, 18432], P('col', 'row')
All inputs are finite; a program needn't handle non-finite values.
Results may differ from a plain program's by a relative error of at most 0.0044.
Values may be sent and summed in bfloat16 or wider, within the bound.
No kernel may reach another device: no remote copies, remote signals or barrier semaphores. Data moves between devices by JAX's collectives and lax.ppermute only.
A program may use at most 64 MiB of HBM per device.

v0:
```python
import jax
import jax.numpy as jnp
from jax import lax
from jax.sharding import Mesh
from jax.sharding import PartitionSpec as P

TL = 64
EXAMPLES = 16
ROW = ("row_0", "row_1", "row_2")


def in_order(tiles, dim):
    tiles = jnp.moveaxis(tiles, 0, dim)
    shape = tiles.shape
    return tiles.reshape(*shape[:dim], shape[dim] * shape[dim + 1], *shape[dim + 2 :])


def copy_for_each(value, axis):
    peers = lax.axis_size(axis)
    return lax.all_to_all(
        jnp.broadcast_to(value[None], (peers, *value.shape)), axis, 0, 0, tiled=True
    )


def gathered_copies(value, axis, dim):
    return in_order(copy_for_each(value, axis), dim)


def in_blocks(value, dim, peers):
    shape = value.shape
    tiles = value.reshape(*shape[:dim], peers, shape[dim] // peers, *shape[dim + 1 :])
    return jnp.moveaxis(tiles, dim, 0)


def sent_and_summed(value, axis, dim):
    tiles = in_blocks(value, dim, lax.axis_size(axis))
    arrived = lax.all_to_all(tiles, axis, split_axis=0, concat_axis=0, tiled=True)
    return arrived.sum(axis=0)


def summed_rows(value, axes, dim):
    far, near = axes
    tiles = in_blocks(value, dim, lax.axis_size(far))
    nearer = sent_and_summed(tiles, near, dim + 1)
    arrived = lax.all_to_all(nearer, far, split_axis=0, concat_axis=0, tiled=True)
    return arrived.sum(axis=0)


def shards(activations, out_grads, query_acts, query_grads, basis_in, basis_out, damping):
    train_act = activations.shape[0]
    block_act = train_act + query_acts.shape[0]
    act_local = jnp.concatenate([activations, query_acts], 0)
    partial_in = jnp.dot(
        lax.all_gather(act_local, ROW, axis=0, tiled=True),
        basis_in,
        preferred_element_type=jnp.float32,
    )
    train_grad = out_grads.shape[0]
    block_grad = train_grad + query_grads.shape[0]
    grad_local = jnp.concatenate([out_grads, query_grads], 0)
    partial_out = jnp.dot(
        gathered_copies(grad_local, "col", 0), basis_out, preferred_element_type=jnp.float32
    )
    share_in = sent_and_summed(partial_in, "col", 0).astype(jnp.bfloat16)
    summed_in = gathered_copies(share_in, "col", 0)
    share_out = summed_rows(partial_out, (("row_0", "row_1"), "row_2"), 0).astype(jnp.bfloat16)
    summed_out = lax.all_gather(share_out, ROW, axis=0, tiled=True)
    width_in = summed_in.shape[1]
    width_out = summed_out.shape[1]
    groups_in = summed_in.reshape(lax.axis_size(ROW), block_act, width_in)
    rot_act = groups_in[:, :train_act].reshape(-1, width_in)
    q_act = groups_in[:, train_act:].reshape(-1, width_in)
    groups_out = summed_out.reshape(lax.axis_size("col"), block_grad, width_out)
    rot_grad = groups_out[:, :train_grad].reshape(-1, width_out)
    q_grad = groups_out[:, train_grad:].reshape(-1, width_out)

    def accumulate(index, total):
        act_block = lax.dynamic_slice_in_dim(rot_act, index * TL, TL, 0)
        grad_block = lax.dynamic_slice_in_dim(rot_grad, index * TL, TL, 0)
        outer = lax.dot_general(
            grad_block, act_block, (((0,), (0,)), ((), ())), preferred_element_type=jnp.float32
        )
        return total + outer * outer

    moment = (
        lax.fori_loop(0, EXAMPLES, accumulate, jnp.zeros((width_out, width_in), jnp.float32))
        / EXAMPLES
    )
    query = lax.dot_general(
        q_grad, q_act, (((0,), (0,)), ((), ())), preferred_element_type=jnp.float32
    )
    return query / (moment + damping[0])


def solution(mesh):
    finer = Mesh(
        mesh.devices.reshape(4, 4, 2, mesh.shape["col"]), ("row_0", "row_1", "row_2", "col")
    )
    placed = (
        P(ROW, "col"),
        P("col", ROW),
        P(ROW, "col"),
        P("col", ROW),
        P("col", ROW),
        P(ROW, "col"),
        P(),
    )
    return jax.shard_map(
        shards, mesh=finer, in_specs=placed, out_specs=P("col", ROW), check_vma=False
    )
```

profile of v0, /device:TPU:1, one launch (start us, length us, event | category | flops | bytes accessed | tf_op | source)
XLA Modules:
  0.0 283.4 jit_solution(13699588076466373404)
XLA Ops:
  6.5 0.0 copy-start
  6.5 0.0 all-gather.7.cloned.1.call-start
  6.5 1.8 maximum_bitcast_fusion
  8.3 0.0 all-gather.7.cloned.1.call-update
  8.3 0.8 copy.21
  9.2 0.8 pad_maximum_fusion
  10.0 0.1 copy.22
  10.2 15.6 %all_to_all.25 = bf16[8,136,224]{2,1,0:T(8,128)(2,1)} all-to-all(bf16[8,136,224]{2,1,0:T(8,128)(2,1)S(1)} %broadcast_in_dim.6), channel_id=1, replica_groups=mesh['row_0'=4,'row_1'=4,'row_2'=2,'col'=8] {'col'}, dimensions={0} | all-to-all | bytes 974848 | tf_op jit(solution)/shard_map/all_to_all | solution.py:20
  25.8 1.4 dot_general.18
  27.2 1.8 convolution_bitcast_fusion
  29.0 1.3 copy.23
  30.3 9.7 %all_to_all.26 = f32[2,16,34,896]{3,1,2,0:T(8,128)} all-to-all(f32[2,16,34,896]{3,1,2,0:T(8,128)S(1)} %copy.23), channel_id=1, replica_groups=mesh['row_0'=4,'row_1'=4,'row_2'=2,'col'=8] {'row_2'}, dimensions={0} | all-to-all | bytes 7798784 | tf_op jit(solution)/shard_map/all_to_all | solution.py:37
  40.0 3.8 %reduce_sum.27 = f32[16,34,896]{2,0,1:T(8,128)} reduce(f32[2,16,34,896]{3,1,2,0:T(8,128)} %all_to_all.26, f32[]{:T(128)} %constant.33.clone.1), dimensions={0}, to_apply=%region_0.0 | reduce | flops 487424 | bytes 5849092 | tf_op jit(solution)/shard_map/reduce_sum | solution.py:38
  43.9 3.5 %copy.24 = f32[16,34,896]{2,1,0:T(8,128)} copy(f32[16,34,896]{2,0,1:T(8,128)} %reduce_sum.27) | data formatting | bytes 3899392 | tf_op jit(solution)/shard_map/reduce_sum | solution.py:38
  47.4 9.9 %all-to-all-start.2 = ((f32[16,34,896]{2,1,0:T(8,128)}), f32[16,34,896]{2,1,0:T(8,128)}, u32[]{:S(2)}, u32[]{:S(2)}) async-start(f32[16,34,896]{2,1,0:T(8,128)} %copy.24), calls=%async_computation.2 | async-start | bytes 4587520 | tf_op jit(solution)/shard_map/all_to_all | solution.py:45
  57.3 53.6 %all-gather.7.cloned.1.call-done = bf16[32,34,2304]{2,1,0:T(8,128)(2,1)} async-done(((bf16[1,34,2304]{2,1,0:T(8,128)(2,1)}), bf16[32,34,2304]{2,1,0:T(8,128)(2,1)}) %all-gather.7.cloned.1.call-update) | async-done | bytes 5013520 | tf_op jit(solution)/shard_map/all_gather | solution.py:54
  110.9 7.8 %reshape.34 = bf16[1088,2304]{1,0:T(8,128)(2,1)} reshape(bf16[32,34,2304]{2,1,0:T(8,128)(2,1)} %all-gather.7.cloned.1.call-done) | data formatting | bytes 10027008
  118.7 0.0 copy-done
  118.7 8.1 %fusion.4 = f32[1088,576]{1,0:T(8,128)} fusion(bf16[1088,2304]{1,0:T(8,128)(2,1)} %reshape.34, bf16[2304,576]{0,1:T(8,128)(2,1)S(1)} %copy-done), kind=kOutput, calls=%fused_computation.11 | convolution fusion | flops 2887778304 | bytes 10174464 | tf_op jit(solution)/shard_map/dot_general | solution.py:53
  126.8 3.0 %all-to-all-done.2 = f32[16,34,896]{2,1,0:T(8,128)} async-done(((f32[16,34,896]{2,1,0:T(8,128)}), f32[16,34,896]{2,1,0:T(8,128)}, u32[]{:S(2)}, u32[]{:S(2)}) %all-to-all-start.2) | async-done | bytes 1949728 | tf_op jit(solution)/shard_map/all_to_all | solution.py:45
  129.7 9.8 %all-to-all-start.3 = ((f32[8,136,576]{2,1,0:T(8,128)}), f32[8,136,576]{2,1,0:T(8,128)}, u32[]{:S(2)}, u32[]{:S(2)}) async-start(f32[8,136,576]{2,1,0:T(8,128)} %bitcast.25), calls=%async_computation.3 | async-start | bytes 5570560 | tf_op jit(solution)/shard_map/all_to_all | solution.py:37
  139.5 0.0 all-gather.5.cloned.1.call-start
  139.6 2.4 reduce_sum.28
  142.0 0.0 all-gather.5.cloned.1.call-update
  142.0 33.7 %all-to-all-done.3 = f32[8,136,576]{2,1,0:T(8,128)} async-done(((f32[8,136,576]{2,1,0:T(8,128)}), f32[8,136,576]{2,1,0:T(8,128)}, u32[]{:S(2)}, u32[]{:S(2)}) %all-to-all-start.3) | async-done | bytes 2506784 | tf_op jit(solution)/shard_map/all_to_all | solution.py:37
  175.7 1.9 reduce_sum.29
  177.6 1.2 broadcast_in_dim.7
  178.8 4.3 %all-to-all-start.4 = ((bf16[8,136,576]{2,1,0:T(8,128)(2,1)}), bf16[8,136,576]{2,1,0:T(8,128)(2,1)}, u32[]{:S(2)}, u32[]{:S(2)}) async-start(bf16[8,136,576]{2,1,0:T(8,128)(2,1)} %broadcast_in_dim.7), calls=%async_computation.4 | async-start | bytes 2785280 | tf_op jit(solution)/shard_map/all_to_all | solution.py:20
  183.8 20.2 %all-gather.5.cloned.1.call-done = bf16[32,34,896]{2,1,0:T(8,128)(2,1)} async-done(((bf16[1,34,896]{2,1,0:T(8,128)(2,1)}), bf16[32,34,896]{2,1,0:T(8,128)(2,1)}) %all-gather.5.cloned.1.call-update) | async-done | bytes 1949712 | tf_op jit(solution)/shard_map/all_gather | solution.py:67
  204.0 4.0 %reshape.25 = bf16[8,136,896]{2,1,0:T(8,128)(2,1)} reshape(bf16[32,34,896]{2,1,0:T(8,128)(2,1)} %all-gather.5.cloned.1.call-done) | data formatting | bytes 3899392 | tf_op jit(solution)/shard_map/reshape | solution.py:73
  208.0 2.9 %slice.18 = bf16[8,128,896]{2,1,0:T(8,128)(2,1)} slice(bf16[8,136,896]{2,1,0:T(8,128)(2,1)} %reshape.25), slice={[0:8], [0:128], [0:896]} | slice | bytes 3670016 | tf_op jit(solution)/shard_map/slice | solution.py:74
  210.8 0.2 all-to-all-done.4
  211.0 3.5 %reshape_reshape.4 = bf16[32,34,576]{2,1,0:T(8,128)(2,1)} reshape(bf16[8,136,576]{2,1,0:T(8,128)(2,1)} %all-to-all-done.4) | data formatting | bytes 2506752 | tf_op jit(solution)/shard_map/reshape;reshape | solution.py:70
  214.6 1.0 slice.17
  215.6 2.5 slice.19
  218.1 0.1 reshape.28
  218.2 55.0 %while.14 = (s32[]{:T(128)}, f32[896,576]{0,1:T(8,128)}, bf16[1024,896]{1,0:T(8,128)(2,1)}, bf16[1024,576]{1,0:T(8,128)(2,1)}, s32[]{:T(128)}, /*index=5*/s32[]{:T(128)}, s32[]{:T(128)}, s32[]{:T(128)}) while((s32[]{:T(128)}, f32[896,576]{0,1:T(8,128)}, bf16[1024,896]{1,0:T(8,128)(2,1)}, bf16[1024,576]{1,0:T(8,128)(2,1)}, ...), condition=%wide.region_4.0_spmd.clone, body=%wide.region_3.0_spmd.clone.sunk | while | flops 67608584 | bytes 4327060 | solution.py:86
  218.2 2.7 select_add_fusion.2
  220.9 3.5 %select_add_fusion.2 = f32[896,576]{0,1:T(8,128)} fusion(f32[896,576]{0,1:T(8,128)} %get-tuple-element.142, pred[]{:T(512)S(6)} %compare.3, bf16[1024,896]{1,0:T(8,128)(2,1)} %get-tuple-element.151, s32[]{:T(128)S(6)} %select_n.10, bf16[1024,576]{1,0:T(8,128)(2,1)} %get-tuple-element.152), kind=kOutput, calls=%fused_computation.clone.1 | convolution fusion | flops 67608576 | bytes 4326912 | tf_op jit(solution)/shard_map/while/body/eval_jaxpr/dot_general | solution.py:80
  224.4 3.5 %select_add_fusion.2 = f32[896,576]{0,1:T(8,128)} fusion(f32[896,576]{0,1:T(8,128)} %get-tuple-element.142, pred[]{:T(512)S(6)} %compare.3, bf16[1024,896]{1,0:T(8,128)(2,1)} %get-tuple-element.151, s32[]{:T(128)S(6)} %select_n.10, bf16[1024,576]{1,0:T(8,128)(2,1)} %get-tuple-element.152), kind=kOutput, calls=%fused_computation.clone.1 | convolution fusion | flops 67608576 | bytes 4326912 | tf_op jit(solution)/shard_map/while/body/eval_jaxpr/dot_general | solution.py:80
  227.9 3.5 %select_add_fusion.2 = f32[896,576]{0,1:T(8,128)} fusion(f32[896,576]{0,1:T(8,128)} %get-tuple-element.142, pred[]{:T(512)S(6)} %compare.3, bf16[1024,896]{1,0:T(8,128)(2,1)} %get-tuple-element.151, s32[]{:T(128)S(6)} %select_n.10, bf16[1024,576]{1,0:T(8,128)(2,1)} %get-tuple-element.152), kind=kOutput, calls=%fused_computation.clone.1 | convolution fusion | flops 67608576 | bytes 4326912 | tf_op jit(solution)/shard_map/while/body/eval_jaxpr/dot_general | solution.py:80
  231.4 3.5 %select_add_fusion.2 = f32[896,576]{0,1:T(8,128)} fusion(f32[896,576]{0,1:T(8,128)} %get-tuple-element.142, pred[]{:T(512)S(6)} %compare.3, bf16[1024,896]{1,0:T(8,128)(2,1)} %get-tuple-element.151, s32[]{:T(128)S(6)} %select_n.10, bf16[1024,576]{1,0:T(8,128)(2,1)} %get-tuple-element.152), kind=kOutput, calls=%fused_computation.clone.1 | convolution fusion | flops 67608576 | bytes 4326912 | tf_op jit(solution)/shard_map/while/body/eval_jaxpr/dot_general | solution.py:80
  234.9 3.5 %select_add_fusion.2 = f32[896,576]{0,1:T(8,128)} fusion(f32[896,576]{0,1:T(8,128)} %get-tuple-element.142, pred[]{:T(512)S(6)} %compare.3, bf16[1024,896]{1,0:T(8,128)(2,1)} %get-tuple-element.151, s32[]{:T(128)S(6)} %select_n.10, bf16[1024,576]{1,0:T(8,128)(2,1)} %get-tuple-element.152), kind=kOutput, calls=%fused_computation.clone.1 | convolution fusion | flops 67608576 | bytes 4326912 | tf_op jit(solution)/shard_map/while/body/eval_jaxpr/dot_general | solution.py:80
  238.3 3.5 %select_add_fusion.2 = f32[896,576]{0,1:T(8,128)} fusion(f32[896,576]{0,1:T(8,128)} %get-tuple-element.142, pred[]{:T(512)S(6)} %compare.3, bf16[1024,896]{1,0:T(8,128)(2,1)} %get-tuple-element.151, s32[]{:T(128)S(6)} %select_n.10, bf16[1024,576]{1,0:T(8,128)(2,1)} %get-tuple-element.152), kind=kOutput, calls=%fused_computation.clone.1 | convolution fusion | flops 67608576 | bytes 4326912 | tf_op jit(solution)/shard_map/while/body/eval_jaxpr/dot_general | solution.py:80
  241.8 3.5 %select_add_fusion.2 = f32[896,576]{0,1:T(8,128)} fusion(f32[896,576]{0,1:T(8,128)} %get-tuple-element.142, pred[]{:T(512)S(6)} %compare.3, bf16[1024,896]{1,0:T(8,128)(2,1)} %get-tuple-element.151, s32[]{:T(128)S(6)} %select_n.10, bf16[1024,576]{1,0:T(8,128)(2,1)} %get-tuple-element.152), kind=kOutput, calls=%fused_computation.clone.1 | convolution fusion | flops 67608576 | bytes 4326912 | tf_op jit(solution)/shard_map/while/body/eval_jaxpr/dot_general | solution.py:80
  245.3 3.5 %select_add_fusion.2 = f32[896,576]{0,1:T(8,128)} fusion(f32[896,576]{0,1:T(8,128)} %get-tuple-element.142, pred[]{:T(512)S(6)} %compare.3, bf16[1024,896]{1,0:T(8,128)(2,1)} %get-tuple-element.151, s32[]{:T(128)S(6)} %select_n.10, bf16[1024,576]{1,0:T(8,128)(2,1)} %get-tuple-element.152), kind=kOutput, calls=%fused_computation.clone.1 | convolution fusion | flops 67608576 | bytes 4326912 | tf_op jit(solution)/shard_map/while/body/eval_jaxpr/dot_general | solution.py:80
  248.8 3.5 %select_add_fusion.2 = f32[896,576]{0,1:T(8,128)} fusion(f32[896,576]{0,1:T(8,128)} %get-tuple-element.142, pred[]{:T(512)S(6)} %compare.3, bf16[1024,896]{1,0:T(8,128)(2,1)} %get-tuple-element.151, s32[]{:T(128)S(6)} %select_n.10, bf16[1024,576]{1,0:T(8,128)(2,1)} %get-tuple-element.152), kind=kOutput, calls=%fused_computation.clone.1 | convolution fusion | flops 67608576 | bytes 4326912 | tf_op jit(solution)/shard_map/while/body/eval_jaxpr/dot_general | solution.py:80
  252.3 3.5 %select_add_fusion.2 = f32[896,576]{0,1:T(8,128)} fusion(f32[896,576]{0,1:T(8,128)} %get-tuple-element.142, pred[]{:T(512)S(6)} %compare.3, bf16[1024,896]{1,0:T(8,128)(2,1)} %get-tuple-element.151, s32[]{:T(128)S(6)} %select_n.10, bf16[1024,576]{1,0:T(8,128)(2,1)} %get-tuple-element.152), kind=kOutput, calls=%fused_computation.clone.1 | convolution fusion | flops 67608576 | bytes 4326912 | tf_op jit(solution)/shard_map/while/body/eval_jaxpr/dot_general | solution.py:80
  255.8 3.5 %select_add_fusion.2 = f32[896,576]{0,1:T(8,128)} fusion(f32[896,576]{0,1:T(8,128)} %get-tuple-element.142, pred[]{:T(512)S(6)} %compare.3, bf16[1024,896]{1,0:T(8,128)(2,1)} %get-tuple-element.151, s32[]{:T(128)S(6)} %select_n.10, bf16[1024,576]{1,0:T(8,128)(2,1)} %get-tuple-element.152), kind=kOutput, calls=%fused_computation.clone.1 | convolution fusion | flops 67608576 | bytes 4326912 | tf_op jit(solution)/shard_map/while/body/eval_jaxpr/dot_general | solution.py:80
  259.2 3.5 %select_add_fusion.2 = f32[896,576]{0,1:T(8,128)} fusion(f32[896,576]{0,1:T(8,128)} %get-tuple-element.142, pred[]{:T(512)S(6)} %compare.3, bf16[1024,896]{1,0:T(8,128)(2,1)} %get-tuple-element.151, s32[]{:T(128)S(6)} %select_n.10, bf16[1024,576]{1,0:T(8,128)(2,1)} %get-tuple-element.152), kind=kOutput, calls=%fused_computation.clone.1 | convolution fusion | flops 67608576 | bytes 4326912 | tf_op jit(solution)/shard_map/while/body/eval_jaxpr/dot_general | solution.py:80
  262.7 3.5 %select_add_fusion.2 = f32[896,576]{0,1:T(8,128)} fusion(f32[896,576]{0,1:T(8,128)} %get-tuple-element.142, pred[]{:T(512)S(6)} %compare.3, bf16[1024,896]{1,0:T(8,128)(2,1)} %get-tuple-element.151, s32[]{:T(128)S(6)} %select_n.10, bf16[1024,576]{1,0:T(8,128)(2,1)} %get-tuple-element.152), kind=kOutput, calls=%fused_computation.clone.1 | convolution fusion | flops 67608576 | bytes 4326912 | tf_op jit(solution)/shard_map/while/body/eval_jaxpr/dot_general | solution.py:80
  266.2 3.5 %select_add_fusion.2 = f32[896,576]{0,1:T(8,128)} fusion(f32[896,576]{0,1:T(8,128)} %get-tuple-element.142, pred[]{:T(512)S(6)} %compare.3, bf16[1024,896]{1,0:T(8,128)(2,1)} %get-tuple-element.151, s32[]{:T(128)S(6)} %select_n.10, bf16[1024,576]{1,0:T(8,128)(2,1)} %get-tuple-element.152), kind=kOutput, calls=%fused_computation.clone.1 | convolution fusion | flops 67608576 | bytes 4326912 | tf_op jit(solution)/shard_map/while/body/eval_jaxpr/dot_general | solution.py:80
  269.7 3.5 %select_add_fusion.2 = f32[896,576]{0,1:T(8,128)} fusion(f32[896,576]{0,1:T(8,128)} %get-tuple-element.142, pred[]{:T(512)S(6)} %compare.3, bf16[1024,896]{1,0:T(8,128)(2,1)} %get-tuple-element.151, s32[]{:T(128)S(6)} %select_n.10, bf16[1024,576]{1,0:T(8,128)(2,1)} %get-tuple-element.152), kind=kOutput, calls=%fused_computation.clone.1 | convolution fusion | flops 67608576 | bytes 4326912 | tf_op jit(solution)/shard_map/while/body/eval_jaxpr/dot_general | solution.py:80
  273.2 3.4 %add_divide_fusion = f32[896,576]{0,1:T(8,128)} fusion(f32[896,576]{0,1:T(8,128)} %get-tuple-element.84, bf16[64,576]{1,0:T(8,128)(2,1)S(1)} %reshape.28, f32[]{:T(128)} %bitcast.23, bf16[8,136,896]{2,1,0:T(8,128)(2,1)} %reshape.25), kind=kOutput, calls=%fused_computation.5 | convolution fusion | flops 67608576 | bytes 4317696 | tf_op jit(solution)/shard_map/dot_general | solution.py:89
  (2 shorter events, 0.0 us)
Async XLA Ops:
  6.5 112.2 %copy-start = (bf16[2304,576]{0,1:T(8,128)(2,1)S(1)}, bf16[2304,576]{0,1:T(8,128)(2,1)}, u32[]{:S(2)}) copy-start(bf16[2304,576]{0,1:T(8,128)(2,1)} %param.13) | copy-start | bytes 7962628
  6.5 104.4 %all-gather.7.cloned.1.call-start = ((), (), s32[]{:S(2)}) async-start(), calls=%async_computation.6 | async-start | bytes 6082560 | tf_op jit(solution)/shard_map/all_gather | solution.py:54
  47.4 82.3 %all-to-all-start.2 = ((f32[16,34,896]{2,1,0:T(8,128)}), f32[16,34,896]{2,1,0:T(8,128)}, u32[]{:S(2)}, u32[]{:S(2)}) async-start(f32[16,34,896]{2,1,0:T(8,128)} %copy.24), calls=%async_computation.2 | async-start | bytes 4587520 | tf_op jit(solution)/shard_map/all_to_all | solution.py:45
  129.7 45.9 %all-to-all-start.3 = ((f32[8,136,576]{2,1,0:T(8,128)}), f32[8,136,576]{2,1,0:T(8,128)}, u32[]{:S(2)}, u32[]{:S(2)}) async-start(f32[8,136,576]{2,1,0:T(8,128)} %bitcast.25), calls=%async_computation.3 | async-start | bytes 5570560 | tf_op jit(solution)/shard_map/all_to_all | solution.py:37
  139.5 64.4 %all-gather.5.cloned.1.call-start = ((), (), s32[]{:S(2)}) async-start(), calls=%async_computation.5 | async-start | bytes 2365440 | tf_op jit(solution)/shard_map/all_gather | solution.py:67
  178.8 32.2 %all-to-all-start.4 = ((bf16[8,136,576]{2,1,0:T(8,128)(2,1)}), bf16[8,136,576]{2,1,0:T(8,128)(2,1)}, u32[]{:S(2)}, u32[]{:S(2)}) async-start(bf16[8,136,576]{2,1,0:T(8,128)(2,1)} %broadcast_in_dim.7), calls=%async_computation.4 | async-start | bytes 2785280 | tf_op jit(solution)/shard_map/all_to_all | solution.py:20
Sparse Core Ops, SparseCore 0:
  10.0 100.9 all-gather.6
  142.9 61.0 all-gather.4
where the time goes:
time: 285 us; the launch traced here: 283 us
  waiting for transfers between devices  111 us (39%)
  matrix products  68.3 us (24%)
  local copies, waits for them, and re-layouts  30.1 us (11%)
  blocking collectives  25.4 us (9%)
  starting transfers between devices  24 us (8%)
  between operations  14.1 us (5%)
  other arithmetic  10.8 us (4%)
    dot_general x16, matrix products, accumulate(): lax.dot_general(grad_block, act_block, (((0,), (0,)), ((), ())), preferre...  55 us
    all_gather x1, waiting for transfers between devices, shards(): lax.all_gather(act_local, ROW, axis=0, tiled=True)  53.6 us
    all_to_all x1, waiting for transfers between devices, sent_and_summed(): lax.all_to_all(tiles, axis, split_axis=0, concat_axis=0, tiled=True)  33.7 us
    all_gather x1, waiting for transfers between devices, shards(): summed_out = lax.all_gather(share_out, ROW, axis=0, tiled=True)  20.2 us
    all_to_all x1, blocking collectives, copy_for_each(): lax.all_to_all(jnp.broadcast_to(value[None], (peers, *value.shape)), axis...  15.6 us
    all_to_all x1, starting transfers between devices, summed_rows(): lax.all_to_all(nearer, far, split_axis=0, concat_axis=0, tiled=True)  9.91 us
    all_to_all x1, starting transfers between devices, sent_and_summed(): lax.all_to_all(tiles, axis, split_axis=0, concat_axis=0, tiled=True)  9.8 us
    all_to_all x1, blocking collectives, sent_and_summed(): lax.all_to_all(tiles, axis, split_axis=0, concat_axis=0, tiled=True)  9.74 us
  transfers between devices with their start and end apart: 5, of which 5 were waited for; matrix products, arithmetic and copies ran while one was open for 15% of the time, Pallas kernels for 0%

commit v1 on v0

v1 whole, which is shorter than its diff:
```python
import functools
import jax
import jax.numpy as jnp
from jax import lax
from jax.experimental import pallas as pl
from jax.experimental.pallas import tpu as pltpu
from jax.sharding import Mesh
from jax.sharding import PartitionSpec as P

EXAMPLES = 16
ROW = ("x", "zh", "core")
COL = ("y", "zl")
BF16 = jnp.bfloat16
WIRE = jnp.float16
F32 = jnp.float32
ROWS = 32
PIECE = 40
TOKENS_FIRST = (((0,), (0,)), ((), ()))


def shifted(value, axis, by):
    size = lax.axis_size(axis)
    return lax.ppermute(value, axis, [(i, (i + by) % size) for i in range(size)])


def swapped(value):
    return shifted(value, "core", 1)


def ring_gather(value, axis):
    back = shifted(value, axis, 1)
    ahead = shifted(value, axis, -1)
    half = value.shape[-1] // 256 * 128
    left = shifted(back[..., :half], axis, 1)
    right = shifted(ahead[..., half:], axis, -1)
    return value, back, ahead, jnp.concatenate([left, right], -1)


def copy_for_each(value, axis):
    peers = lax.axis_size(axis)
    return lax.all_to_all(
        jnp.broadcast_to(value[None], (peers, *value.shape)), axis, 0, 0, tiled=True
    )


def padded(value, rows):
    return jnp.pad(value, ((0, rows - value.shape[0]), (0, 0)))


def summed_share(partial, axis, scale):
    arrived = lax.all_to_all((partial * scale).astype(WIRE), axis, 0, 0, tiled=True)
    return (arrived.astype(F32).sum(0) * (1 / scale)).astype(BF16)


def final_kernel(place, damping, act_own, act_other, grad_own, grad_other, out):
    core, x, zh = place[0], place[1], place[2]
    first = core == 0
    height, width = out.shape
    tile = 256

    for left in range(0, width, tile):
        cols = slice(left, min(left + tile, width))

        def in_turn(own, other):
            return [jnp.where(first, own, other), jnp.where(first, other, own)]

        total = None
        query_act, query_grad = [], []
        for block in range(EXAMPLES // 2):
            for source, part in ((grad_own, core), (grad_other, 1 - core)):
                example = 2 * block + part
                slot_x = (example // 4 - x + 4) % 4
                slot_z = (example % 4 - zh + 4) % 4
                slot_x = jnp.where(slot_x == 0, 0, slot_x % 3 + 1)
                slot_z = jnp.where(slot_z == 0, 0, slot_z % 3 + 1)
                slot = slot_x * 4 + slot_z
                act = jnp.concatenate(
                    in_turn(act_own[slot, :ROWS, cols], act_other[slot, :ROWS, cols]), 0
                )
                grad = jnp.concatenate(
                    [source[2 * block, :ROWS, :], source[2 * block + 1, :ROWS, :]], 0
                )
                outer = lax.dot_general(grad, act, TOKENS_FIRST, preferred_element_type=F32)
                total = outer * outer if total is None else total + outer * outer
                query_act += in_turn(act_own[slot, ROWS:, cols], act_other[slot, ROWS:, cols])
                query_grad += [source[2 * block, ROWS:, :], source[2 * block + 1, ROWS:, :]]
        query = lax.dot_general(
            jnp.concatenate(query_grad, 0),
            jnp.concatenate(query_act, 0),
            TOKENS_FIRST,
            preferred_element_type=F32,
        )
        out[:, cols] = query / (total * (1 / EXAMPLES) + damping[0])


def corrected(place, damping, act_own, act_other, grad_own, grad_other):
    width, height = act_own.shape[2], grad_own.shape[2]
    return pl.pallas_call(
        final_kernel,
        out_shape=jax.ShapeDtypeStruct((height, width), F32),
        in_specs=[pl.BlockSpec(memory_space=pltpu.SMEM)] * 2
        + [pl.BlockSpec(memory_space=pltpu.VMEM)] * 4,
        out_specs=pl.BlockSpec(memory_space=pltpu.VMEM),
        compiler_params=pltpu.CompilerParams(vmem_limit_bytes=40 * 2**20),
        name="corrected",
    )(place, damping, act_own, act_other, grad_own, grad_other)


def shards(activations, out_grads, query_acts, query_grads, basis_in, basis_out, damping):
    core = lax.axis_index("core")
    width_in = basis_in.shape[1]
    width_out = basis_out.shape[1]

    basis_in_both = jnp.concatenate([basis_in, swapped(basis_in)], 1)
    basis_out_both = jnp.concatenate([basis_out, swapped(basis_out)], 0)

    acts = jnp.concatenate([activations, query_acts, jnp.zeros((6, activations.shape[1]), BF16)], 0)
    along_z = jnp.stack(ring_gather(acts, "zh"))
    along_x = jnp.concatenate(ring_gather(along_z, "x"), 0)
    gathered_in = along_x.reshape(-1, acts.shape[1])

    def half(which):
        rows = out_grads.shape[0] // 2
        q_rows = query_grads.shape[0] // 2
        train = lax.dynamic_slice_in_dim(out_grads, which * rows, rows, 0)
        query = lax.dynamic_slice_in_dim(query_grads, which * q_rows, q_rows, 0)
        pieces = []
        for i in range(2):
            pieces.append(train[i * ROWS : (i + 1) * ROWS])
            pieces.append(padded(query[i * 2 : (i + 1) * 2], PIECE - ROWS))
        return jnp.concatenate(pieces, 0)

    grads = jnp.concatenate([half(core), swapped(half(1 - core))], 1)
    gathered_out = copy_for_each(grads, COL).reshape(-1, grads.shape[1])

    partial_out = jnp.dot(gathered_out, basis_out_both, preferred_element_type=F32)
    share_out = summed_share(partial_out.reshape(16, PIECE, width_out), ("x", "zh"), 2.0**11)
    grad_own = copy_for_each(share_out, "zh")
    grad_own = copy_for_each(grad_own, "x").reshape(16, PIECE, width_out)
    grad_other = swapped(grad_own)

    partial_in = jnp.dot(gathered_in, basis_in_both, preferred_element_type=F32)
    share_in = summed_share(partial_in.reshape(8, 2 * PIECE, 2 * width_in), COL, 2.0**6)
    act_both = copy_for_each(share_in, COL).reshape(16, PIECE, 2 * width_in)
    act_own = act_both[:, :, :width_in]
    act_other = swapped(act_both[:, :, width_in:])

    place = jnp.stack([core, lax.axis_index("x"), lax.axis_index("zh")]).astype(jnp.int32)
    return corrected(place, damping, act_own, act_other, grad_own, grad_other)


def solution(mesh):
    finer = Mesh(mesh.devices.reshape(4, 4, 2, 4, 2), (*ROW, *COL))
    placed = (
        P(ROW, COL),
        P(COL, ROW),
        P(ROW, COL),
        P(COL, ROW),
        P(COL, ROW),
        P(ROW, COL),
        P(),
    )
    return jax.shard_map(
        shards, mesh=finer, in_specs=placed, out_specs=P(COL, ROW), check_vma=False
    )
```

time: 285 us -> 191 us (0.67)
  matrix products: 68.3 us -> 10.5 us
  waiting for transfers between devices: 111 us -> 58.4 us
  starting transfers between devices: 24 us -> 59.9 us
  between operations: 14.1 us -> 0.89 us
  Pallas kernels: 0 us -> 6.02 us
  blocking collectives: 25.4 us -> 19.5 us
  other arithmetic: 10.8 us -> 5.25 us
    all_gather x2 -> x0, waiting for transfers between devices: 73.8 us -> none  [the longest x1 53.6 us: shards(): lax.all_gather(act_local, ROW, axis=0, tiled=True)]
    dot_general x19 -> x2, matrix products: 68.3 us -> 10.5 us  [the longest x1 8.67 us: shards(): partial_in = jnp.dot(gathered_in, basis_in_both, preferred_element_type=F32)]
    ppermute x0 -> x13, waiting for transfers between devices: none -> 41.8 us  [shifted(): lax.ppermute(value, axis, [(i, (i + by) % size) for i in range(size)])]
    all_to_all x2 -> x1, waiting for transfers between devices: 36.6 us -> 0.01 us  [summed_share(): lax.all_to_all((partial * scale).astype(WIRE), axis, 0, 0, tiled=True)]
    ppermute x0 -> x13, starting transfers between devices: none -> 33.3 us  [shifted(): lax.ppermute(value, axis, [(i, (i + by) % size) for i in range(size)])]
    all_to_all x1 -> x4, waiting for transfers between devices: 0.19 us -> 16.6 us  [copy_for_each(): lax.all_to_all(jnp.broadcast_to(value[None], (peers, *value.shape)), axis...]
    all_to_all x1 -> x4, starting transfers between devices: 4.28 us -> 19.5 us  [copy_for_each(): lax.all_to_all(jnp.broadcast_to(value[None], (peers, *value.shape)), axis...]
    all_to_all x2 -> x1, starting transfers between devices: 19.7 us -> 7.13 us  [summed_share(): lax.all_to_all((partial * scale).astype(WIRE), axis, 0, 0, tiled=True)]
  transfers between devices with their start and end apart: 5 -> 18, of which waited for: 5 -> 9; matrix products, arithmetic and copies ran while one was open for 15% -> 18% of each run, Pallas kernels for 0% -> 0%
where the time goes in v1:
time: 191 us; the launch traced here: 190 us
  starting transfers between devices  59.9 us (31%)
  waiting for transfers between devices  58.4 us (31%)
  local copies, waits for them, and re-layouts  29.5 us (15%)
  blocking collectives  19.5 us (10%)
  matrix products  10.5 us (5%)
  Pallas kernels  6.02 us (3%)
  other arithmetic  5.25 us (3%)
    ppermute x13, waiting for transfers between devices, shifted(): lax.ppermute(value, axis, [(i, (i + by) % size) for i in range(size)])  41.8 us
    ppermute x13, starting transfers between devices, shifted(): lax.ppermute(value, axis, [(i, (i + by) % size) for i in range(size)])  33.3 us
    all_to_all x4, starting transfers between devices, copy_for_each(): lax.all_to_all(jnp.broadcast_to(value[None], (peers, *value.shape)), axis...  19.5 us
    all_to_all x1, blocking collectives, summed_share(): lax.all_to_all((partial * scale).astype(WIRE), axis, 0, 0, tiled=True)  19.5 us
    all_to_all x4, waiting for transfers between devices, copy_for_each(): lax.all_to_all(jnp.broadcast_to(value[None], (peers, *value.shape)), axis...  16.6 us
    unnamed x21, local copies, waits for them, and re-layouts  13.9 us
    dot_general x1, matrix products, shards(): partial_in = jnp.dot(gathered_in, basis_in_both, preferred_element_type=F32)  8.67 us
    all_to_all x1, starting transfers between devices, summed_share(): lax.all_to_all((partial * scale).astype(WIRE), axis, 0, 0, tiled=True)  7.13 us
  transfers between devices with their start and end apart: 18, of which 9 were waited for; matrix products, arithmetic and copies ran while one was open for 18% of the time, Pallas kernels for 0%

profile of v1, /device:TPU:1, one launch (start us, length us, event | category | flops | bytes accessed | tf_op | source)
XLA Modules:
  0.0 190.0 jit_solution(967936862331849170)
XLA Ops:
  0.1 1.0 fusion.25
  1.1 3.9 %collective-permute-start = (bf16[40,2304]{1,0:T(8,128)(2,1)S(1)}, bf16[40,2304]{1,0:T(8,128)(2,1)S(1)}, u32[]{:S(2)}, u32[]{:S(2)}) collective-permute-start(bf16[40,2304]{1,0:T(8,128)(2,1)S(1)} %get-tuple-element.8), channel_id=1, source_target_pairs={{0,16},{16,32},{32,48},{48,0},{1,17},{17,33},{33,49},{49,1},{2,18}... | collective-permute-start | bytes 552968 | tf_op jit(solution)/shard_map/ppermute | solution.py:23
  5.0 3.1 %collective-permute-start.1 = (bf16[40,2304]{1,0:T(8,128)(2,1)S(1)}, bf16[40,2304]{1,0:T(8,128)(2,1)S(1)}, u32[]{:S(2)}, u32[]{:S(2)}) collective-permute-start(bf16[40,2304]{1,0:T(8,128)(2,1)S(1)} %get-tuple-element.8), channel_id=1, source_target_pairs={{0,48},{16,0},{32,16},{48,32},{1,49},{17,1},{33,17},{49,33},{2,50}... | collective-permute-start | bytes 552968 | tf_op jit(solution)/shard_map/ppermute | solution.py:23
  8.1 1.0 collective-permute-start.8
  9.1 0.8 constant_dynamic-slice_fusion.2
  9.9 0.2 copy.27
  10.1 0.2 copy.26
  10.3 1.1 constant_dynamic-slice_fusion.3
  11.4 0.1 fusion.22
  11.5 0.1 collective-permute-start.10
  11.6 0.5 collective-permute-start.11
  12.1 1.7 constant_dynamic-update-slice_fusion.5
  13.8 4.5 %copy.16 = bf16[2304,576]{1,0:T(8,128)(2,1)} copy(bf16[2304,576]{0,1:T(8,128)(2,1)} %param.11) | data formatting | bytes 5308416 | tf_op args[4]
  18.3 0.2 copy.25
  18.5 0.2 copy.24
  18.7 0.1 pad_maximum_fusion.1
  18.8 0.1 copy.22
  18.9 0.9 broadcast_in_dim.12
  19.8 4.7 %all-to-all-start.2 = ((bf16[8,80,448]{2,1,0:T(8,128)(2,1)}), bf16[8,80,448]{2,1,0:T(8,128)(2,1)S(1)}, u32[]{:S(2)}, u32[]{:S(2)}) async-start(bf16[8,80,448]{2,1,0:T(8,128)(2,1)} %broadcast_in_dim.12), calls=%async_computation.2 | async-start | bytes 1310720 | tf_op jit(solution)/shard_map/all_to_all | solution.py:41
  24.5 2.6 %collective-permute-start.3 = (bf16[40,1152]{1,0:T(8,128)(2,1)S(1)}, bf16[40,1152]{1,0:T(8,128)(2,1)S(1)}, u32[]{:S(2)}, u32[]{:S(2)}) collective-permute-start(bf16[40,1152]{1,0:T(8,128)(2,1)S(1)} %slice.57), channel_id=1, source_target_pairs={{0,48},{16,0},{32,16},{48,32},{1,49},{17,1},{33,17},{49,33},{2,50}... | collective-permute-start | bytes 276488 | tf_op jit(solution)/shard_map/ppermute | solution.py:23
  27.2 0.1 collective-permute-start.2
  27.2 0.7 constant_dynamic-update-slice_fusion.4
  27.9 1.5 collective-permute-done.3
  29.4 9.6 %collective-permute-done.2 = bf16[40,1152]{1,0:T(8,128)(2,1)S(1)} collective-permute-done((bf16[40,1152]{1,0:T(8,128)(2,1)S(1)}, bf16[40,1152]{1,0:T(8,128)(2,1)S(1)}, u32[]{:S(2)}, u32[]{:S(2)}) %collective-permute-start.2) | collective-permute-done | bytes 92192 | tf_op jit(solution)/shard_map/ppermute | solution.py:23
  39.1 1.9 multiply_convert_fusion
  40.9 7.1 %all-to-all-start.3 = ((f16[16,40,896]{2,1,0:T(8,128)(2,1)}), f16[16,40,896]{2,1,0:T(8,128)(2,1)S(1)}, u32[]{:S(2)}, u32[]{:S(2)}) async-start(f16[16,40,896]{2,1,0:T(8,128)(2,1)} %multiply_convert_fusion), calls=%async_computation.3 | async-start | bytes 2293760 | tf_op jit(solution)/shard_map/all_to_all | solution.py:51
  48.1 0.1 pad_maximum_fusion
  48.2 1.4 collective-permute-start.4
  49.6 1.3 collective-permute-start.5
  50.9 0.7 constant_dynamic-update-slice_fusion.3
  51.6 0.7 constant_dynamic-update-slice_fusion.2
  52.3 23.4 %collective-permute-done.5 = bf16[4,40,2304]{2,1,0:T(8,128)(2,1)S(1)} collective-permute-done((bf16[4,40,2304]{2,1,0:T(8,128)(2,1)S(1)}, bf16[4,40,2304]{2,1,0:T(8,128)(2,1)S(1)}, u32[]{:S(2)}, u32[]{:S(2)}) %collective-permute-start.5) | collective-permute-done | bytes 737312 | tf_op jit(solution)/shard_map/ppermute | solution.py:23
  75.8 3.6 %collective-permute-start.7 = (bf16[4,40,1152]{2,1,0:T(8,128)(2,1)S(1)}, bf16[4,40,1152]{2,1,0:T(8,128)(2,1)S(1)}, u32[]{:S(2)}, u32[]{:S(2)}) collective-permute-start(bf16[4,40,1152]{2,1,0:T(8,128)(2,1)S(1)} %slice.59), channel_id=1, source_target_pairs={{0,192},{64,0},{128,64},{192,128},{1,193},{65,1},{129,65},{193,129... | collective-permute-start | bytes 1105928 | tf_op jit(solution)/shard_map/ppermute | solution.py:23
  79.4 0.1 collective-permute-start.6
  79.5 0.9 constant_dynamic-update-slice_fusion.1
  80.4 1.0 constant_dynamic-update-slice_fusion
  81.4 3.6 %collective-permute-done.7 = bf16[4,40,1152]{2,1,0:T(8,128)(2,1)S(1)} collective-permute-done((bf16[4,40,1152]{2,1,0:T(8,128)(2,1)S(1)}, bf16[4,40,1152]{2,1,0:T(8,128)(2,1)S(1)}, u32[]{:S(2)}, u32[]{:S(2)}) %collective-permute-start.7) | collective-permute-done | bytes 368672 | tf_op jit(solution)/shard_map/ppermute | solution.py:23
  85.1 3.2 %collective-permute-done.6 = bf16[4,40,1152]{2,1,0:T(8,128)(2,1)S(1)} collective-permute-done((bf16[4,40,1152]{2,1,0:T(8,128)(2,1)S(1)}, bf16[4,40,1152]{2,1,0:T(8,128)(2,1)S(1)}, u32[]{:S(2)}, u32[]{:S(2)}) %collective-permute-start.6) | collective-permute-done | bytes 368672 | tf_op jit(solution)/shard_map/ppermute | solution.py:23
  88.3 1.0 maximum_dynamic-update-slice_fusion
  89.3 4.5 %copy.17 = bf16[2304,576]{1,0:T(8,128)(2,1)} copy(bf16[2304,576]{0,1:T(8,128)(2,1)} %collective-permute-done.8) | data formatting | bytes 5308416 | tf_op jit(solution)/shard_map/ppermute | solution.py:23
  93.8 0.2 convert_reduce_fusion.1
  94.0 0.7 broadcast_in_dim.13
  94.7 7.0 %all-to-all-start.4 = ((bf16[4,40,896]{2,1,0:T(8,128)(2,1)}), bf16[4,40,896]{2,1,0:T(8,128)(2,1)S(1)}, u32[]{:S(2)}, u32[]{:S(2)}) async-start(bf16[4,40,896]{2,1,0:T(8,128)(2,1)} %broadcast_in_dim.13), calls=%async_computation.4 | async-start | bytes 573440 | tf_op jit(solution)/shard_map/all_to_all | solution.py:41
  101.7 8.7 %fusion.4 = f16[8,80,1152]{2,1,0:T(8,128)(2,1)} fusion(bf16[8,80,2304]{2,1,0:T(8,128)(2,1)} %bitcast.35, bf16[2304,576]{1,0:T(8,128)(2,1)} %copy.17, bf16[2304,576]{1,0:T(8,128)(2,1)} %copy.16), kind=kOutput, calls=%fused_computation.5 | convolution fusion | flops 3409477632 | bytes 9732096 | tf_op jit(solution)/shard_map/dot_general | solution.py:142
  110.4 0.2 all-to-all-done.4
  110.6 19.5 %all_to_all.30 = f16[8,80,1152]{2,1,0:T(8,128)(2,1)S(1)} all-to-all(f16[8,80,1152]{2,1,0:T(8,128)(2,1)} %fusion.4), channel_id=1, replica_groups=mesh['x'=4,'zh'=4,'core'=2,'y'=4,'zl'=2] {'y','zl'}, dimensions={0} | all-to-all | bytes 2949120 | tf_op jit(solution)/shard_map/all_to_all | solution.py:51
  130.0 1.1 broadcast_in_dim.14
  131.1 3.5 %all-to-all-start.5 = ((bf16[4,4,40,896]{3,2,1,0:T(8,128)(2,1)}), bf16[4,4,40,896]{3,2,1,0:T(8,128)(2,1)S(1)}, u32[]{:S(2)}, u32[]{:S(2)}) async-start(bf16[4,4,40,896]{3,2,1,0:T(8,128)(2,1)} %broadcast_in_dim.14), calls=%async_computation.5 | async-start | bytes 2293760 | tf_op jit(solution)/shard_map/all_to_all | solution.py:41
  134.7 0.2 convert_reduce_fusion
  134.9 10.0 %all-to-all-done.5 = bf16[4,4,40,896]{3,2,1,0:T(8,128)(2,1)S(1)} async-done(((bf16[4,4,40,896]{3,2,1,0:T(8,128)(2,1)}), bf16[4,4,40,896]{3,2,1,0:T(8,128)(2,1)S(1)}, u32[]{:S(2)}, u32[]{:S(2)}) %all-to-all-start.5) | async-done | bytes 1146912 | tf_op jit(solution)/shard_map/all_to_all | solution.py:41
  144.9 1.2 broadcast_in_dim.11
  146.1 4.3 %all-to-all-start.1 = ((bf16[8,80,1152]{2,1,0:T(8,128)(2,1)}), bf16[8,80,1152]{2,1,0:T(8,128)(2,1)}, u32[]{:S(2)}, u32[]{:S(2)}) async-start(bf16[8,80,1152]{2,1,0:T(8,128)(2,1)} %broadcast_in_dim.11), calls=%async_computation.1 | async-start | bytes 2949120 | tf_op jit(solution)/shard_map/all_to_all | solution.py:41
  150.4 6.9 %collective-permute-start.12 = (bf16[16,40,896]{2,1,0:T(8,128)(2,1)S(1)}, bf16[16,40,896]{2,1,0:T(8,128)(2,1)S(1)}, u32[]{:S(2)}, u32[]{:S(2)}) collective-permute-start(bf16[16,40,896]{2,1,0:T(8,128)(2,1)S(1)} %bitcast.30), channel_id=1, source_target_pairs={{0,8},{8,0},{1,9},{9,1},{2,10},{10,2},{3,11},{11,3},{4,12},{12,4},... | collective-permute-start | bytes 3440648 | tf_op jit(solution)/shard_map/ppermute | solution.py:23
  157.4 6.4 %all-to-all-done.1 = bf16[8,80,1152]{2,1,0:T(8,128)(2,1)} async-done(((bf16[8,80,1152]{2,1,0:T(8,128)(2,1)}), bf16[8,80,1152]{2,1,0:T(8,128)(2,1)}, u32[]{:S(2)}, u32[]{:S(2)}) %all-to-all-start.1) | async-done | bytes 1474592 | tf_op jit(solution)/shard_map/all_to_all | solution.py:41
  163.7 3.0 %fusion.26 = (bf16[16,40,576]{2,1,0:T(8,128)(2,1)}, bf16[16,40,576]{2,1,0:T(8,128)(2,1)}) fusion(bf16[16,40,1152]{2,1,0:T(8,128)(2,1)} %bitcast.9), kind=kLoop, calls=%fused_computation.60 | loop fusion | bytes 2949120 | tf_op jit(solution)/shard_map/slice | solution.py:146
  166.7 8.7 %collective-permute-start.9 = (bf16[16,40,576]{2,1,0:T(8,128)(2,1)}, bf16[16,40,576]{2,1,0:T(8,128)(2,1)S(1)}, u32[]{:S(2)}, u32[]{:S(2)}) collective-permute-start(bf16[16,40,576]{2,1,0:T(8,128)(2,1)} %get-tuple-element.5), channel_id=1, source_target_pairs={{0,8},{8,0},{1,9},{9,1},{2,10},{10,2},{3,11},{11,3},{4,12},{12,4},... | collective-permute-start | bytes 2211848 | tf_op jit(solution)/shard_map/ppermute | solution.py:23
  176.1 1.0 copy-done.1
  177.1 0.4 collective-permute-done.9.act_other
  177.5 0.9 copy-done.3
  178.4 1.1 copy-done
  179.6 1.3 copy-done.2
  180.8 1.1 copy-done.4
  182.0 6.0 %corrected.1 = f32[896,576]{1,0:T(8,128)S(1)} custom-call(s32[3]{0:T(128)S(1)} %pad_add_fusion.place, f32[1]{0:T(128)S(6)} %copy.34.damping, bf16[16,40,576]{2,1,0:T(8,128)(2,1)S(1)} %copy-done, bf16[16,40,576]{2,1,0:T(8,128)(2,1)S(1)} %copy-done.4, bf16[16,40,896]{2,1,0:T(8,128)(2,1)S(1)} %bitcast.31, bf16[16,40,896]{2,1,0:T(8,128)(2,1)S(1)} %copy-done.2), custom_call_target="tpu_custom_call" | custom-call | tf_op jit(solution)/shard_map/corrected/pallas_call | solution.py:98
  188.0 2.0 %copy.23 = f32[896,576]{0,1:T(8,128)} copy(f32[896,576]{1,0:T(8,128)S(1)} %corrected.1) | data formatting | bytes 4128768 | tf_op jit(solution)/shard_map/corrected/pallas_call | solution.py:98
  (26 shorter events, 0.3 us)
Async XLA Ops:
  1.1 26.0 %collective-permute-start = (bf16[40,2304]{1,0:T(8,128)(2,1)S(1)}, bf16[40,2304]{1,0:T(8,128)(2,1)S(1)}, u32[]{:S(2)}, u32[]{:S(2)}) collective-permute-start(bf16[40,2304]{1,0:T(8,128)(2,1)S(1)} %get-tuple-element.8), channel_id=1, source_target_pairs={{0,16},{16,32},{32,48},{48,0},{1,17},{17,33},{33,49},{49,1},{2,18}... | collective-permute-start | bytes 552968 | tf_op jit(solution)/shard_map/ppermute | solution.py:23
  5.0 19.5 %collective-permute-start.1 = (bf16[40,2304]{1,0:T(8,128)(2,1)S(1)}, bf16[40,2304]{1,0:T(8,128)(2,1)S(1)}, u32[]{:S(2)}, u32[]{:S(2)}) collective-permute-start(bf16[40,2304]{1,0:T(8,128)(2,1)S(1)} %get-tuple-element.8), channel_id=1, source_target_pairs={{0,48},{16,0},{32,16},{48,32},{1,49},{17,1},{33,17},{49,33},{2,50}... | collective-permute-start | bytes 552968 | tf_op jit(solution)/shard_map/ppermute | solution.py:23
  8.1 81.2 %collective-permute-start.8 = (bf16[2304,576]{0,1:T(8,128)(2,1)}, bf16[2304,576]{0,1:T(8,128)(2,1)}, u32[]{:S(2)}, u32[]{:S(2)}) collective-permute-start(bf16[2304,576]{0,1:T(8,128)(2,1)} %param.11), channel_id=1, source_target_pairs={{0,8},{8,0},{1,9},{9,1},{2,10},{10,2},{3,11},{11,3},{4,12},{12,4},... | collective-permute-start | bytes 7962632 | tf_op jit(solution)/shard_map/ppermute | solution.py:23
  11.5 7.2 %collective-permute-start.10 = (bf16[80,224]{0,1:T(8,128)(2,1)S(1)}, bf16[80,224]{0,1:T(8,128)(2,1)S(1)}, u32[]{:S(2)}, u32[]{:S(2)}) collective-permute-start(bf16[80,224]{0,1:T(8,128)(2,1)S(1)} %fusion.22), channel_id=1, source_target_pairs={{0,8},{8,0},{1,9},{9,1},{2,10},{10,2},{3,11},{11,3},{4,12},{12,4},... | collective-permute-start | bytes 107528 | tf_op jit(solution)/shard_map/ppermute | solution.py:23
  11.6 27.4 %collective-permute-start.11 = (bf16[224,896]{1,0:T(8,128)(2,1)}, bf16[224,896]{1,0:T(8,128)(2,1)S(1)}, u32[]{:S(2)}, u32[]{:S(2)}) collective-permute-start(bf16[224,896]{1,0:T(8,128)(2,1)} %param.12), channel_id=1, source_target_pairs={{0,8},{8,0},{1,9},{9,1},{2,10},{10,2},{3,11},{11,3},{4,12},{12,4},... | collective-permute-start | bytes 1204232 | tf_op jit(solution)/shard_map/ppermute | solution.py:23
  18.3 20.7 %copy-start.5 = (bf16[224,896]{1,0:T(8,128)(2,1)S(1)}, bf16[224,896]{1,0:T(8,128)(2,1)}, u32[]{:S(2)}) copy-start(bf16[224,896]{1,0:T(8,128)(2,1)} %param.12) | copy-start | bytes 1204228
  19.8 19.2 %all-to-all-start.2 = ((bf16[8,80,448]{2,1,0:T(8,128)(2,1)}), bf16[8,80,448]{2,1,0:T(8,128)(2,1)S(1)}, u32[]{:S(2)}, u32[]{:S(2)}) async-start(bf16[8,80,448]{2,1,0:T(8,128)(2,1)} %broadcast_in_dim.12), calls=%async_computation.2 | async-start | bytes 1310720 | tf_op jit(solution)/shard_map/all_to_all | solution.py:41
  24.5 4.9 %collective-permute-start.3 = (bf16[40,1152]{1,0:T(8,128)(2,1)S(1)}, bf16[40,1152]{1,0:T(8,128)(2,1)S(1)}, u32[]{:S(2)}, u32[]{:S(2)}) collective-permute-start(bf16[40,1152]{1,0:T(8,128)(2,1)S(1)} %slice.57), channel_id=1, source_target_pairs={{0,48},{16,0},{32,16},{48,32},{1,49},{17,1},{33,17},{49,33},{2,50}... | collective-permute-start | bytes 276488 | tf_op jit(solution)/shard_map/ppermute | solution.py:23
  27.2 11.9 %collective-permute-start.2 = (bf16[40,1152]{1,0:T(8,128)(2,1)S(1)}, bf16[40,1152]{1,0:T(8,128)(2,1)S(1)}, u32[]{:S(2)}, u32[]{:S(2)}) collective-permute-start(bf16[40,1152]{1,0:T(8,128)(2,1)S(1)} %slice.56), channel_id=1, source_target_pairs={{0,16},{16,32},{32,48},{48,0},{1,17},{17,33},{33,49},{49,1},{2,18}... | collective-permute-start | bytes 276488 | tf_op jit(solution)/shard_map/ppermute | solution.py:23
  40.9 52.8 %all-to-all-start.3 = ((f16[16,40,896]{2,1,0:T(8,128)(2,1)}), f16[16,40,896]{2,1,0:T(8,128)(2,1)S(1)}, u32[]{:S(2)}, u32[]{:S(2)}) async-start(f16[16,40,896]{2,1,0:T(8,128)(2,1)} %multiply_convert_fusion), calls=%async_computation.3 | async-start | bytes 2293760 | tf_op jit(solution)/shard_map/all_to_all | solution.py:51
  48.2 31.2 %collective-permute-start.4 = (bf16[4,40,2304]{2,1,0:T(8,128)(2,1)S(1)}, bf16[4,40,2304]{2,1,0:T(8,128)(2,1)S(1)}, u32[]{:S(2)}, u32[]{:S(2)}) collective-permute-start(bf16[4,40,2304]{2,1,0:T(8,128)(2,1)S(1)} %pad_maximum_fusion), channel_id=1, source_target_pairs={{0,64},{64,128},{128,192},{192,0},{1,65},{65,129},{129,193},{193,1... | collective-permute-start | bytes 2211848 | tf_op jit(solution)/shard_map/ppermute | solution.py:23
  49.6 26.1 %collective-permute-start.5 = (bf16[4,40,2304]{2,1,0:T(8,128)(2,1)S(1)}, bf16[4,40,2304]{2,1,0:T(8,128)(2,1)S(1)}, u32[]{:S(2)}, u32[]{:S(2)}) collective-permute-start(bf16[4,40,2304]{2,1,0:T(8,128)(2,1)S(1)} %pad_maximum_fusion), channel_id=1, source_target_pairs={{0,192},{64,0},{128,64},{192,128},{1,193},{65,1},{129,65},{193,129... | collective-permute-start | bytes 2211848 | tf_op jit(solution)/shard_map/ppermute | solution.py:23
  75.8 9.3 %collective-permute-start.7 = (bf16[4,40,1152]{2,1,0:T(8,128)(2,1)S(1)}, bf16[4,40,1152]{2,1,0:T(8,128)(2,1)S(1)}, u32[]{:S(2)}, u32[]{:S(2)}) collective-permute-start(bf16[4,40,1152]{2,1,0:T(8,128)(2,1)S(1)} %slice.59), channel_id=1, source_target_pairs={{0,192},{64,0},{128,64},{192,128},{1,193},{65,1},{129,65},{193,129... | collective-permute-start | bytes 1105928 | tf_op jit(solution)/shard_map/ppermute | solution.py:23
  79.4 8.9 %collective-permute-start.6 = (bf16[4,40,1152]{2,1,0:T(8,128)(2,1)S(1)}, bf16[4,40,1152]{2,1,0:T(8,128)(2,1)S(1)}, u32[]{:S(2)}, u32[]{:S(2)}) collective-permute-start(bf16[4,40,1152]{2,1,0:T(8,128)(2,1)S(1)} %slice.58), channel_id=1, source_target_pairs={{0,64},{64,128},{128,192},{192,0},{1,65},{65,129},{129,193},{193,1... | collective-permute-start | bytes 1105928 | tf_op jit(solution)/shard_map/ppermute | solution.py:23
  94.7 15.9 %all-to-all-start.4 = ((bf16[4,40,896]{2,1,0:T(8,128)(2,1)}), bf16[4,40,896]{2,1,0:T(8,128)(2,1)S(1)}, u32[]{:S(2)}, u32[]{:S(2)}) async-start(bf16[4,40,896]{2,1,0:T(8,128)(2,1)} %broadcast_in_dim.13), calls=%async_computation.4 | async-start | bytes 573440 | tf_op jit(solution)/shard_map/all_to_all | solution.py:41
  131.1 13.8 %all-to-all-start.5 = ((bf16[4,4,40,896]{3,2,1,0:T(8,128)(2,1)}), bf16[4,4,40,896]{3,2,1,0:T(8,128)(2,1)S(1)}, u32[]{:S(2)}, u32[]{:S(2)}) async-start(bf16[4,4,40,896]{3,2,1,0:T(8,128)(2,1)} %broadcast_in_dim.14), calls=%async_computation.5 | async-start | bytes 2293760 | tf_op jit(solution)/shard_map/all_to_all | solution.py:41
  146.1 17.6 %all-to-all-start.1 = ((bf16[8,80,1152]{2,1,0:T(8,128)(2,1)}), bf16[8,80,1152]{2,1,0:T(8,128)(2,1)}, u32[]{:S(2)}, u32[]{:S(2)}) async-start(bf16[8,80,1152]{2,1,0:T(8,128)(2,1)} %broadcast_in_dim.11), calls=%async_computation.1 | async-start | bytes 2949120 | tf_op jit(solution)/shard_map/all_to_all | solution.py:41
  150.4 25.7 %collective-permute-start.12 = (bf16[16,40,896]{2,1,0:T(8,128)(2,1)S(1)}, bf16[16,40,896]{2,1,0:T(8,128)(2,1)S(1)}, u32[]{:S(2)}, u32[]{:S(2)}) collective-permute-start(bf16[16,40,896]{2,1,0:T(8,128)(2,1)S(1)} %bitcast.30), channel_id=1, source_target_pairs={{0,8},{8,0},{1,9},{9,1},{2,10},{10,2},{3,11},{11,3},{4,12},{12,4},... | collective-permute-start | bytes 3440648 | tf_op jit(solution)/shard_map/ppermute | solution.py:23
  166.7 10.9 %collective-permute-start.9 = (bf16[16,40,576]{2,1,0:T(8,128)(2,1)}, bf16[16,40,576]{2,1,0:T(8,128)(2,1)S(1)}, u32[]{:S(2)}, u32[]{:S(2)}) collective-permute-start(bf16[16,40,576]{2,1,0:T(8,128)(2,1)} %get-tuple-element.5), channel_id=1, source_target_pairs={{0,8},{8,0},{1,9},{9,1},{2,10},{10,2},{3,11},{11,3},{4,12},{12,4},... | collective-permute-start | bytes 2211848 | tf_op jit(solution)/shard_map/ppermute | solution.py:23
  176.1 1.0 copy-start.1
  177.5 0.9 copy-start.3
  178.4 1.1 copy-start
  179.6 1.3 copy-start.2
  180.8 1.1 copy-start.4

commit v2 on v1

v2 whole, which is shorter than its diff:
```python
import functools
import jax
import jax.numpy as jnp
from jax import lax
from jax.experimental import pallas as pl
from jax.experimental.pallas import tpu as pltpu
from jax.sharding import Mesh
from jax.sharding import PartitionSpec as P

EXAMPLES = 16
ROW = ("x", "zh", "core")
COL = ("y", "zl")
BF16 = jnp.bfloat16
WIRE = jnp.float16
F32 = jnp.float32
SCALE_IN = 2.0**6
SCALE_OUT = 2.0**11
SCALE_OUT_X = 2.0**9
TOKENS_FIRST = (((0,), (0,)), ((), ()))
LAST_LAST = (((1,), (1,)), ((), ()))
VMEM = pl.BlockSpec(memory_space=pltpu.VMEM)
SMEM = pl.BlockSpec(memory_space=pltpu.SMEM)
ANY = pl.BlockSpec(memory_space=pl.ANY)
HBM = pl.BlockSpec(memory_space=pltpu.HBM)


NO_COST = pl.CostEstimate(flops=0, bytes_accessed=0, transcendentals=0)


def params(mib):
    return pltpu.CompilerParams(vmem_limit_bytes=mib * 2**20)


def from_ahead(value, axis, by):
    size = lax.axis_size(axis)
    return lax.ppermute(value, axis, [((i + by) % size, i) for i in range(size)])


def swapped(value):
    return from_ahead(value, "core", 1)


def exchanged(blocks, axis):
    return lax.all_to_all(blocks, axis, 0, 0, tiled=True)


def shares_kernel(place, own, other, earlier, out):
    first = place[0] == 0
    lower = jnp.where(first, own[...], other[...])
    upper = jnp.where(first, other[...], own[...])
    for peer in range(out.shape[0]):
        out[peer, 0] = lower
        out[peer, 1] = upper


def shares_for_each(place, own, other, peers, earlier):
    return pl.pallas_call(
        shares_kernel,
        out_shape=jax.ShapeDtypeStruct((peers, 2, *own.shape), own.dtype),
        in_specs=[SMEM, VMEM, VMEM, ANY],
        out_specs=VMEM,
        cost_estimate=NO_COST,
        compiler_params=params(4),
        name="shares",
    )(place, own, other, earlier)


def both_kernel(own, other, earlier, out):
    for peer in range(out.shape[0]):
        out[peer, 0] = own[...]
        out[peer, 1] = other[...]


def both_for_each(own, other, peers, earlier):
    return pl.pallas_call(
        both_kernel,
        out_shape=jax.ShapeDtypeStruct((peers, 2, *own.shape), own.dtype),
        in_specs=[VMEM, VMEM, ANY],
        out_specs=VMEM,
        cost_estimate=NO_COST,
        compiler_params=params(4),
        name="both",
    )(own, other, earlier)


def copied(moves, sem):
    handles = [pltpu.make_async_copy(*move, sem.at[i]) for i, move in enumerate(moves)]
    for handle in handles:
        handle.start()
    for handle in handles:
        handle.wait()


def step_call(kernel, shapes, moves, operands, name):
    return pl.pallas_call(
        kernel,
        out_shape=tuple(jax.ShapeDtypeStruct(shape, BF16) for shape in shapes),
        in_specs=[HBM] * len(operands),
        out_specs=(HBM,) * len(shapes),
        scratch_shapes=[pltpu.SemaphoreType.DMA((moves,))],
        cost_estimate=NO_COST,
        compiler_params=params(2),
        name=name,
    )(*operands)


def sides_kernel(ahead, back, earlier, left, right, sem):
    half = left.shape[2]
    copied([(ahead.at[:, :, :half], left), (back.at[:, :, half:], right)], sem)


def sides(ahead, back, earlier):
    count, rows, width = ahead.shape
    part = (count, rows, width // 2)
    return step_call(sides_kernel, [part, part], 2, [ahead, back, earlier], "sides")


def along_kernel(own, ahead, left, right, back, out, sem):
    half = left.shape[2]
    copied(
        [
            (own, out.at[0:1]),
            (ahead, out.at[1:2]),
            (left, out.at[2:3, :, :half]),
            (right, out.at[2:3, :, half:]),
            (back, out.at[3:4]),
        ],
        sem,
    )


def along(own, ahead, left, right, back):
    shape = (4, *own.shape[1:])
    return step_call(along_kernel, [shape], 5, [own, ahead, left, right, back], "along")[0]


def halves_kernel(place, grads, query, keep, send):
    core = place[0]
    train = grads[...].astype(F32).T
    rows = lax.broadcasted_iota(jnp.int32, query.shape, 0)
    wide = query[...].astype(F32)

    def half(which):
        parts = []
        for i in range(2):
            by = 2 * which + 2 * i
            rolled = wide if by == 0 else jnp.concatenate([wide[by:], wide[:by]], 0)
            mine = (rows >= 2 * which) & (rows < 2 * which + 2)
            start = 64 * which + 32 * i
            parts += [train[start : start + 32], jnp.where(mine, rolled, 0.0)]
        return jnp.concatenate(parts, 0)

    lower, upper = half(0), half(1)
    keep[...] = jnp.where(core == 0, lower, upper).astype(BF16)
    send[...] = jnp.where(core == 0, upper, lower).astype(BF16)


def token_halves(place, grads, query):
    shape = jax.ShapeDtypeStruct((80, grads.shape[1]), BF16)
    return pl.pallas_call(
        halves_kernel,
        out_shape=(shape, shape),
        in_specs=[SMEM, VMEM, VMEM],
        out_specs=(VMEM, VMEM),
        cost_estimate=NO_COST,
        compiler_params=params(4),
        name="token_halves",
    )(place, grads.T, query)


def rotate_out_kernel(place, tokens, basis_own, basis_other, earlier, out):
    x = place[1]
    width = tokens.shape[3]
    for part in range(4):
        rows = slice(2 * part, 2 * part + 2)
        product = jnp.dot(
            tokens[rows, 0].reshape(-1, width), basis_own[...], preferred_element_type=F32
        ) + jnp.dot(
            tokens[rows, 1].reshape(-1, width), basis_other[...], preferred_element_type=F32
        )
        product = (product * SCALE_OUT).reshape(4, 40, -1)
        for z in range(4):
            out[(part - x + 4) % 4, z] = product[z]


def rotated_out(place, tokens, basis_own, basis_other, earlier):
    width = basis_own.shape[1]
    return pl.pallas_call(
        rotate_out_kernel,
        out_shape=jax.ShapeDtypeStruct((4, 4, 40, width), F32),
        in_specs=[SMEM, VMEM, VMEM, VMEM, ANY],
        out_specs=VMEM,
        cost_estimate=NO_COST,
        compiler_params=params(6),
        name="rotated_out",
    )(place, tokens, basis_own, basis_other, earlier)


def rotate_in_kernel(count, place, earlier, *refs):
    pieces, (own, other) = refs[:count], refs[count : count + 2]
    out, tokens, queries, basis, sem = refs[count + 2 :]
    zh = place[2]
    width, depth = own.shape
    half = depth // 2
    moves, at = [], 0
    for piece in pieces:
        blocks = piece.shape[0]
        if piece.shape[2] == depth:
            moves.append((piece, tokens.at[at : at + blocks]))
            at += blocks
        elif len(moves) % 2 == 0:
            moves.append((piece, tokens.at[at : at + blocks, :, :half]))
        else:
            moves.append((piece, tokens.at[at : at + blocks, :, half:]))
            at += blocks
    moves.append((own, basis.at[:width]))
    moves.append((other, basis.at[width:]))
    handles = [pltpu.make_async_copy(*move, sem.at[i]) for i, move in enumerate(moves)]
    for handle in handles:
        handle.start()
    for handle in handles[:-1]:
        handle.wait()
    for group in range(at // 4):
        for pair in range(2):
            first, second = ((2 * pair + i - zh + 4) % 4 for i in range(2))
            queries[2 * group + pair] = (
                tokens[4 * group + first, 32:, :].astype(F32)
                + tokens[4 * group + second, 32:, :].astype(F32)
            )
    rows = jnp.concatenate(
        [tokens[:, :32, :].reshape(-1, depth), queries[...].reshape(-1, depth).astype(BF16)], 0
    )
    split = at * 32
    for start in range(0, 2 * width, 256):
        stop = min(start + 256, 2 * width)
        if start < width < stop:
            handles[-1].wait()
        product = lax.dot_general(rows, basis[start:stop, :], LAST_LAST, preferred_element_type=F32)
        product = product * SCALE_IN
        out[:, :64, start:stop] = product[:split].reshape(-1, 64, stop - start)
        out[:, 64:, start:stop] = product[split:].reshape(-1, 8, stop - start)


def rotated_in(place, pieces, own, other, earlier):
    count = len(pieces)
    width, depth = own.shape
    blocks = sum(piece.size for piece in pieces) // (40 * depth)
    return pl.pallas_call(
        functools.partial(rotate_in_kernel, count),
        out_shape=jax.ShapeDtypeStruct((blocks // 2, 72, 2 * width), F32),
        in_specs=[SMEM, ANY] + [HBM] * (count + 2),
        out_specs=VMEM,
        scratch_shapes=[
            pltpu.VMEM((blocks, 40, depth), BF16),
            pltpu.VMEM((blocks // 2, 8, depth), F32),
            pltpu.VMEM((2 * width, depth), BF16),
            pltpu.SemaphoreType.DMA((count + 2,)),
        ],
        cost_estimate=NO_COST,
        compiler_params=params(24),
        name="rotated_in",
    )(place, earlier, *pieces, own, other)


def final_kernel(place, damping, acts, *refs):
    grads_own, grads_other, out = refs[:4], refs[4:8], refs[8]
    core, x, zh = place[0], place[1], place[2]
    width, height = out.shape
    tile = 192

    for left in range(0, width, tile):
        cols = slice(left, min(left + tile, width))
        total = None
        query_act, query_grad = [], []
        for step in range(4):
            for pair in range(2):
                places = [(2 * pair + half - zh + 4) % 4 for half in range(2)]
                for source, part in ((grads_own[step], core), (grads_other[step], 1 - core)):
                    slot = (2 * pair + part - zh + 4) % 4
                    share = 2 * step + slot // 2
                    rows = pl.ds(pl.multiple_of(slot % 2 * 32, 32), 32)
                    act = jnp.concatenate([acts[share, half, rows, cols] for half in range(2)], 0)
                    grad = jnp.concatenate([source[at, :32, :] for at in places], 0)
                    outer = lax.dot_general(act, grad, TOKENS_FIRST, preferred_element_type=F32)
                    total = outer * outer if total is None else total + outer * outer
                for half, at in enumerate(places):
                    query_act.append(acts[2 * step + pair, half, 64:, cols])
                    query_grad.append(grads_own[step][at, 32:, :] + grads_other[step][at, 32:, :])
        query = lax.dot_general(
            jnp.concatenate(query_act, 0),
            jnp.concatenate(query_grad, 0),
            TOKENS_FIRST,
            preferred_element_type=F32,
        )
        out[cols, :] = query / (total * (1 / EXAMPLES) + damping[0])


def corrected(place, damping, acts, grads_own, grads_other):
    shape = (acts.shape[3], grads_own[0].shape[2])
    return pl.pallas_call(
        final_kernel,
        out_shape=jax.ShapeDtypeStruct(shape, F32),
        in_specs=[SMEM, SMEM] + [VMEM] * 9,
        out_specs=VMEM,
        cost_estimate=NO_COST,
        compiler_params=params(12),
        name="corrected",
    )(place, damping, acts, *grads_own, *grads_other)


def shards(activations, out_grads, query_acts, query_grads, basis_in, basis_out, damping):
    core, x, zh = (lax.axis_index(name) for name in ROW[2:] + ROW[:2])
    place = jnp.stack([core, x, zh]).astype(jnp.int32)
    width_in = basis_in.shape[1]

    group = jnp.where(
        zh % 2 == 0,
        jnp.pad(query_acts, ((0, 6), (0, 0))),
        jnp.pad(query_acts, ((2, 4), (0, 0))),
    )
    own = jnp.concatenate([activations, group], 0)[None]
    z_ahead = from_ahead(own, "zh", 1)
    z_back = from_ahead(own, "zh", -1)

    columns_own = basis_in.T
    columns_other = swapped(columns_own)
    basis_out_other = swapped(basis_out)

    keep, send = token_halves(place, out_grads, query_grads)
    received = swapped(send)

    left, right = sides(z_ahead, z_back, received)
    z_left = from_ahead(left, "zh", 1)
    z_right = from_ahead(right, "zh", -1)
    row = along(own, z_ahead, z_left, z_right, z_back)
    x_ahead = from_ahead(row, "x", 1)
    x_back = from_ahead(row, "x", -1)

    grads = exchanged(both_for_each(keep, received, 8, row), COL)
    partial_out = rotated_out(place, grads, basis_out, basis_out_other, row)

    left, right = sides(x_ahead, x_back, partial_out)
    x_left = from_ahead(left, "x", 1)
    x_right = from_ahead(right, "x", -1)

    early = rotated_in(place, [row, x_ahead, x_back], columns_own, columns_other, left)
    late = rotated_in(place, [x_left, x_right], columns_own, columns_other, early)
    partial_in = jnp.concatenate([early[:4], late, early[4:]], 0).astype(WIRE)
    arrived_in = exchanged(partial_in, COL)

    wire_out = partial_out[1:].astype(WIRE)
    sum_x = partial_out[0]
    for by in range(1, 4):
        sum_x = sum_x + from_ahead(wire_out[by - 1], "x", -by).astype(F32)
    sum_x = sum_x * (SCALE_OUT_X / SCALE_OUT)
    share_out = lax.dynamic_index_in_dim(sum_x, zh, 0, False)
    for by in range(1, 4):
        block = lax.dynamic_index_in_dim(sum_x, (zh + by) % 4, 0, False).astype(WIRE)
        share_out = share_out + from_ahead(block, "zh", -by).astype(F32)
    share_out = (share_out * (1 / SCALE_OUT_X)).astype(BF16)
    blocks = [share_out] + [from_ahead(share_out, "zh", by) for by in range(1, 4)]
    blocks = jnp.stack(blocks)
    grads_own = [blocks] + [from_ahead(blocks, "x", by) for by in range(1, 4)]
    grads_other = [swapped(value) for value in grads_own]

    share_in = (arrived_in.astype(F32).sum(0) * (1 / SCALE_IN)).astype(BF16)
    own = share_in[:, :width_in]
    other = swapped(share_in[:, width_in:])
    acts = exchanged(shares_for_each(place, own, other, 8, blocks), COL)

    return corrected(place, damping, acts, grads_own, grads_other).T


def solution(mesh):
    finer = Mesh(mesh.devices.reshape(4, 4, 2, 4, 2), (*ROW, *COL))
    placed = (
        P(ROW, COL),
        P(COL, ROW),
        P(ROW, COL),
        P(COL, ROW),
        P(COL, ROW),
        P(ROW, COL),
        P(),
    )
    return jax.shard_map(
        shards, mesh=finer, in_specs=placed, out_specs=P(COL, ROW), check_vma=False
    )
```

time: 191 us -> 150 us (0.79)
  local copies, waits for them, and re-layouts: 29.5 us -> 7.29 us
  waiting for transfers between devices: 58.4 us -> 36.9 us
  blocking collectives: 19.5 us -> 0 us
  Pallas kernels: 6.02 us -> 23.4 us
  starting transfers between devices: 59.9 us -> 74.6 us
  matrix products: 10.5 us -> 0 us
    ppermute x13 -> x28, starting transfers between devices: 33.3 us -> 56.9 us  [from_ahead(): lax.ppermute(value, axis, [((i + by) % size, i) for i in range(size)])]
    all_to_all x1 -> x0, blocking collectives: 19.5 us -> none  [summed_share(): lax.all_to_all((partial * scale).astype(WIRE), axis, 0, 0, tiled=True)]
    pallas_call x1 -> x10, Pallas kernels: 6.02 us -> 23.4 us  [the longest x2 9.93 us: rotated_in(): pl.pallas_call(functools.partial(rotate_in_kernel, count), out_shape=jax....]
    all_to_all x5 -> x3, waiting for transfers between devices: 16.6 us -> 3.19 us  [exchanged(): return lax.all_to_all(blocks, axis, 0, 0, tiled=True)]
    dot_general x2 -> x0, matrix products: 10.5 us -> none  [the longest x1 8.67 us: shards(): partial_in = jnp.dot(gathered_in, basis_in_both, preferred_element_type=F32)]
    all_to_all x5 -> x3, starting transfers between devices: 26.6 us -> 17.7 us  [exchanged(): return lax.all_to_all(blocks, axis, 0, 0, tiled=True)]
    ppermute x13 -> x28, waiting for transfers between devices: 41.8 us -> 33.7 us  [from_ahead(): lax.ppermute(value, axis, [((i + by) % size, i) for i in range(size)])]
    unnamed x21 -> x20, local copies, waits for them, and re-layouts: 13.9 us -> 6.88 us
  transfers between devices with their start and end apart: 18 -> 31, of which waited for: 9 -> 17; matrix products, arithmetic and copies ran while one was open for 18% -> 4% of each run, Pallas kernels for 0% -> 7%
where the time goes in v2:
time: 150 us; the launch traced here: 149 us
  starting transfers between devices  74.6 us (50%)
  waiting for transfers between devices  36.9 us (25%)
  Pallas kernels  23.4 us (16%)
  local copies, waits for them, and re-layouts  7.29 us (5%)
  other arithmetic  6.45 us (4%)
    ppermute x28, starting transfers between devices, from_ahead(): lax.ppermute(value, axis, [((i + by) % size, i) for i in range(size)])  56.9 us
    ppermute x28, waiting for transfers between devices, from_ahead(): lax.ppermute(value, axis, [((i + by) % size, i) for i in range(size)])  33.7 us
    all_to_all x3, starting transfers between devices, exchanged(): return lax.all_to_all(blocks, axis, 0, 0, tiled=True)  17.7 us
    pallas_call x2, Pallas kernels, rotated_in(): pl.pallas_call(functools.partial(rotate_in_kernel, count), out_shape=jax....  9.93 us
    unnamed x20, local copies, waits for them, and re-layouts  6.88 us
    pallas_call x1, Pallas kernels, corrected(): pl.pallas_call(final_kernel, out_shape=jax.ShapeDtypeStruct(shape, F32),...  6.84 us
    all_to_all x3, waiting for transfers between devices, exchanged(): return lax.all_to_all(blocks, axis, 0, 0, tiled=True)  3.19 us
  transfers between devices with their start and end apart: 31, of which 17 were waited for; matrix products, arithmetic and copies ran while one was open for 4% of the time, Pallas kernels for 7%

profile of v2, /device:TPU:1, one launch (start us, length us, event | category | flops | bytes accessed | tf_op | source)
XLA Modules:
  0.0 149.5 jit_solution(2162447776233766565)
XLA Ops:
  0.0 3.2 %collective-permute-start.8 = (bf16[576,2304]{1,0:T(8,128)(2,1)}, bf16[576,2304]{1,0:T(8,128)(2,1)}, u32[]{:S(2)}, u32[]{:S(2)}) collective-permute-start(bf16[576,2304]{1,0:T(8,128)(2,1)} %bitcast.44), channel_id=1, source_target_pairs={{8,0},{0,8},{9,1},{1,9},{10,2},{2,10},{11,3},{3,11},{12,4},{4,12},... | collective-permute-start | bytes 7962632 | tf_op jit(solution)/shard_map/ppermute | solution.py:36
  3.2 0.8 pad_select_fusion
  4.0 0.9 maximum_bitcast_fusion.own
  5.0 4.4 %collective-permute-start = (bf16[1,40,2304]{2,1,0:T(8,128)(2,1)S(1)}, bf16[1,40,2304]{2,1,0:T(8,128)(2,1)S(1)}, u32[]{:S(2)}, u32[]{:S(2)}) collective-permute-start(bf16[1,40,2304]{2,1,0:T(8,128)(2,1)S(1)} %maximum_bitcast_fusion.own), channel_id=1, source_target_pairs={{16,0},{32,16},{48,32},{0,48},{17,1},{33,17},{49,33},{1,49},{18,2}... | collective-permute-start | bytes 552968 | tf_op jit(solution)/shard_map/ppermute | solution.py:36
  9.4 0.8 copy-done.8
  10.2 0.7 copy-done.9
  10.9 0.6 token_halves.1
  11.6 0.4 collective-permute-start.2
  11.9 0.9 collective-permute-done.2.earlier.other
  12.9 3.5 %collective-permute-done.ahead = bf16[1,40,2304]{2,1,0:T(8,128)(2,1)S(1)} collective-permute-done((bf16[1,40,2304]{2,1,0:T(8,128)(2,1)S(1)}, bf16[1,40,2304]{2,1,0:T(8,128)(2,1)S(1)}, u32[]{:S(2)}, u32[]{:S(2)}) %collective-permute-start) | collective-permute-done | bytes 184352 | tf_op jit(solution)/shard_map/ppermute | solution.py:36
  16.3 1.8 %collective-permute-done.1.back = bf16[1,40,2304]{2,1,0:T(8,128)(2,1)S(1)} collective-permute-done((bf16[1,40,2304]{2,1,0:T(8,128)(2,1)S(1)}, bf16[1,40,2304]{2,1,0:T(8,128)(2,1)S(1)}, u32[]{:S(2)}, u32[]{:S(2)}) %collective-permute-start.1) | collective-permute-done | bytes 184352 | tf_op jit(solution)/shard_map/ppermute | solution.py:36
  18.2 1.4 collective-permute-start.3
  19.6 1.0 collective-permute-start.4
  20.6 1.9 %collective-permute-done.3.left = bf16[1,40,1152]{2,1,0:T(8,128)(2,1)S(1)} collective-permute-done((bf16[1,40,1152]{2,1,0:T(8,128)(2,1)S(1)}, bf16[1,40,1152]{2,1,0:T(8,128)(2,1)S(1)}, u32[]{:S(2)}, u32[]{:S(2)}) %collective-permute-start.3) | collective-permute-done | bytes 92192 | tf_op jit(solution)/shard_map/ppermute | solution.py:36
  22.6 2.6 %collective-permute-done.4.right = bf16[1,40,1152]{2,1,0:T(8,128)(2,1)S(1)} collective-permute-done((bf16[1,40,1152]{2,1,0:T(8,128)(2,1)S(1)}, bf16[1,40,1152]{2,1,0:T(8,128)(2,1)S(1)}, u32[]{:S(2)}, u32[]{:S(2)}) %collective-permute-start.4) | collective-permute-done | bytes 92192 | tf_op jit(solution)/shard_map/ppermute | solution.py:36
  25.1 0.8 along.1.earlier.refs_0_
  25.9 0.9 both.1
  26.8 8.2 %all-to-all-start = ((bf16[8,2,80,224]{3,2,1,0:T(8,128)(2,1)}), bf16[8,2,80,224]{3,2,1,0:T(8,128)(2,1)S(1)}, u32[]{:S(2)}, u32[]{:S(2)}) async-start(bf16[8,2,80,224]{3,2,1,0:T(8,128)(2,1)} %both.1), calls=%async_computation | async-start | bytes 1310720 | tf_op jit(solution)/shard_map/all_to_all | solution.py:44
  35.0 2.5 %collective-permute-start.5 = (bf16[4,40,2304]{2,1,0:T(8,128)(2,1)S(1)}, bf16[4,40,2304]{2,1,0:T(8,128)(2,1)}, u32[]{:S(2)}, u32[]{:S(2)}) collective-permute-start(bf16[4,40,2304]{2,1,0:T(8,128)(2,1)S(1)} %along.1.earlier.refs_0_), channel_id=1, source_target_pairs={{64,0},{128,64},{192,128},{0,192},{65,1},{129,65},{193,129},{1,193... | collective-permute-start | bytes 2211848 | tf_op jit(solution)/shard_map/ppermute | solution.py:36
  37.5 2.0 %collective-permute-start.7 = (bf16[224,896]{1,0:T(8,128)(2,1)S(1)}, bf16[224,896]{1,0:T(8,128)(2,1)S(1)}, u32[]{:S(2)}, u32[]{:S(2)}) collective-permute-start(bf16[224,896]{1,0:T(8,128)(2,1)S(1)} %copy-done.3), channel_id=1, source_target_pairs={{8,0},{0,8},{9,1},{1,9},{10,2},{2,10},{11,3},{3,11},{12,4},{4,12},... | collective-permute-start | bytes 1204232 | tf_op jit(solution)/shard_map/ppermute | solution.py:36
  39.5 1.4 collective-permute-done.7.basis_other
  40.9 0.8 copy-done.4
  41.6 3.2 %all-to-all-done.tokens = bf16[8,2,80,224]{3,2,1,0:T(8,128)(2,1)S(1)} async-done(((bf16[8,2,80,224]{3,2,1,0:T(8,128)(2,1)}), bf16[8,2,80,224]{3,2,1,0:T(8,128)(2,1)S(1)}, u32[]{:S(2)}, u32[]{:S(2)}) %all-to-all-start) | async-done | bytes 573472 | tf_op jit(solution)/shard_map/all_to_all | solution.py:44
  44.8 0.8 copy-done.1
  45.7 1.1 copy-done.2
  46.7 1.0 copy-done.5
  47.7 1.4 rotated_out.1.earlier
  49.1 2.4 %collective-permute-done.5.ahead.refs_1_ = bf16[4,40,2304]{2,1,0:T(8,128)(2,1)} collective-permute-done((bf16[4,40,2304]{2,1,0:T(8,128)(2,1)S(1)}, bf16[4,40,2304]{2,1,0:T(8,128)(2,1)}, u32[]{:S(2)}, u32[]{:S(2)}) %collective-permute-start.5) | collective-permute-done | bytes 737312 | tf_op jit(solution)/shard_map/ppermute | solution.py:36
  51.6 3.2 %collective-permute-done.6.back.refs_2_ = bf16[4,40,2304]{2,1,0:T(8,128)(2,1)} collective-permute-done((bf16[4,40,2304]{2,1,0:T(8,128)(2,1)S(1)}, bf16[4,40,2304]{2,1,0:T(8,128)(2,1)}, u32[]{:S(2)}, u32[]{:S(2)}) %collective-permute-start.6) | collective-permute-done | bytes 737312 | tf_op jit(solution)/shard_map/ppermute | solution.py:36
  54.8 1.1 sides.3
  56.0 2.7 %collective-permute-start.9 = (bf16[4,40,1152]{2,1,0:T(8,128)(2,1)S(1)}, bf16[4,40,1152]{2,1,0:T(8,128)(2,1)S(1)}, u32[]{:S(2)}, u32[]{:S(2)}) collective-permute-start(bf16[4,40,1152]{2,1,0:T(8,128)(2,1)S(1)} %get-tuple-element.15.earlier), channel_id=1, source_target_pairs={{64,0},{128,64},{192,128},{0,192},{65,1},{129,65},{193,129},{1,193... | collective-permute-start | bytes 1105928 | tf_op jit(solution)/shard_map/ppermute | solution.py:36
  58.7 6.1 %rotated_in.2.earlier = f32[6,72,1152]{2,1,0:T(8,128)S(1)} custom-call(s32[3]{0:T(128)S(1)} %pad_add_fusion.place, bf16[4,40,1152]{2,1,0:T(8,128)(2,1)S(1)} %get-tuple-element.15.earlier, bf16[4,40,2304]{2,1,0:T(8,128)(2,1)S(1)} %along.1.earlier.refs_0_, bf16[4,40,2304]{2,1,0:T(8,128)(2,1)} %collective-permute-done.5.ahead.refs_1_, ...), custom_call_target="tpu_custom_call" | custom-call | tf_op jit(solution)/shard_map/rotated_in/pallas_call | solution.py:248
  65.1 3.8 %rotated_in.3 = f32[2,72,1152]{2,1,0:T(8,128)S(1)} custom-call(s32[3]{0:T(128)S(1)} %pad_add_fusion.place, f32[6,72,1152]{2,1,0:T(8,128)S(1)} %rotated_in.2.earlier, bf16[4,40,1152]{2,1,0:T(8,128)(2,1)S(1)} %collective-permute-done.9.refs_0_, bf16[4,40,1152]{2,1,0:T(8,128)(2,1)S(1)} %collective-permute-done.10.refs_1_, bf16[576,2304]{1,0:T(8,128)(2,1)S(1)} %bitcast.46, ...), custom_call_target="tpu_custom_call" | custom-call | tf_op jit(solution)/shard_map/rotated_in/pallas_call | solution.py:248
  69.0 1.4 pad_maximum_fusion
  70.4 4.9 %all-to-all-start.1 = ((f16[8,72,1152]{2,1,0:T(8,128)(2,1)}), f16[8,72,1152]{2,1,0:T(8,128)(2,1)}, u32[]{:S(2)}, u32[]{:S(2)}) async-start(f16[8,72,1152]{2,1,0:T(8,128)(2,1)} %pad_maximum_fusion), calls=%async_computation.1 | async-start | bytes 2654208 | tf_op jit(solution)/shard_map/all_to_all | solution.py:44
  75.3 0.1 convert.14
  75.4 0.1 slice_bitcast_fusion.3
  75.7 2.3 %collective-permute-start.13 = (f16[4,40,896]{2,1,0:T(8,128)(2,1)S(1)}, f16[4,40,896]{2,1,0:T(8,128)(2,1)}, u32[]{:S(2)}, u32[]{:S(2)}) collective-permute-start(f16[4,40,896]{2,1,0:T(8,128)(2,1)S(1)} %get-tuple-element.19), channel_id=1, source_target_pairs={{128,0},{192,64},{0,128},{64,192},{129,1},{193,65},{1,129},{65,193... | collective-permute-start | bytes 860168 | tf_op jit(solution)/shard_map/ppermute | solution.py:36
  78.0 0.4 collective-permute-start.14
  78.3 7.4 %collective-permute-done.12 = f16[4,40,896]{2,1,0:T(8,128)(2,1)S(1)} collective-permute-done((f16[4,40,896]{2,1,0:T(8,128)(2,1)S(1)}, f16[4,40,896]{2,1,0:T(8,128)(2,1)S(1)}, u32[]{:S(2)}, u32[]{:S(2)}) %collective-permute-start.12) | collective-permute-done | bytes 286752 | tf_op jit(solution)/shard_map/ppermute | solution.py:36
  85.8 0.2 collective-permute-done.13
  86.0 2.8 %collective-permute-done.14 = f16[4,40,896]{2,1,0:T(8,128)(2,1)} collective-permute-done((f16[4,40,896]{2,1,0:T(8,128)(2,1)S(1)}, f16[4,40,896]{2,1,0:T(8,128)(2,1)}, u32[]{:S(2)}, u32[]{:S(2)}) %collective-permute-start.14) | collective-permute-done | bytes 286752 | tf_op jit(solution)/shard_map/ppermute | solution.py:36
  88.8 1.2 fusion.3
  90.2 4.6 %collective-permute-start.16 = (f16[40,896]{1,0:T(8,128)(2,1)S(1)}, f16[40,896]{1,0:T(8,128)(2,1)S(1)}, u32[]{:S(2)}, u32[]{:S(2)}) collective-permute-start(f16[40,896]{1,0:T(8,128)(2,1)S(1)} %get-tuple-element.22), channel_id=1, source_target_pairs={{32,0},{48,16},{0,32},{16,48},{33,1},{49,17},{1,33},{17,49},{34,2}... | collective-permute-start | bytes 215048 | tf_op jit(solution)/shard_map/ppermute | solution.py:36
  94.8 0.6 collective-permute-done.15
  95.4 2.4 %collective-permute-done.16 = f16[40,896]{1,0:T(8,128)(2,1)S(1)} collective-permute-done((f16[40,896]{1,0:T(8,128)(2,1)S(1)}, f16[40,896]{1,0:T(8,128)(2,1)S(1)}, u32[]{:S(2)}, u32[]{:S(2)}) %collective-permute-start.16) | collective-permute-done | bytes 71712 | tf_op jit(solution)/shard_map/ppermute | solution.py:36
  97.8 1.1 collective-permute-done.17
  99.0 2.1 %collective-permute-start.18 = (bf16[40,896]{1,0:T(8,128)(2,1)S(1)}, bf16[40,896]{1,0:T(8,128)(2,1)S(1)}, u32[]{:S(2)}, u32[]{:S(2)}) collective-permute-start(bf16[40,896]{1,0:T(8,128)(2,1)S(1)} %fusion.7), channel_id=1, source_target_pairs={{16,0},{32,16},{48,32},{0,48},{17,1},{33,17},{49,33},{1,49},{18,2}... | collective-permute-start | bytes 215048 | tf_op jit(solution)/shard_map/ppermute | solution.py:36
  101.1 4.1 %collective-permute-start.19 = (bf16[40,896]{1,0:T(8,128)(2,1)S(1)}, bf16[40,896]{1,0:T(8,128)(2,1)S(1)}, u32[]{:S(2)}, u32[]{:S(2)}) collective-permute-start(bf16[40,896]{1,0:T(8,128)(2,1)S(1)} %fusion.7), channel_id=1, source_target_pairs={{32,0},{48,16},{0,32},{16,48},{33,1},{49,17},{1,33},{17,49},{34,2}... | collective-permute-start | bytes 215048 | tf_op jit(solution)/shard_map/ppermute | solution.py:36
  105.2 0.6 collective-permute-start.20
  105.8 1.5 %convert_reduce_fusion = f32[72,1152]{1,0:T(8,128)S(1)} fusion(f16[8,72,1152]{2,1,0:T(8,128)(2,1)} %all-to-all-done.1), kind=kLoop, calls=%fused_computation | loop fusion | flops 1244160 | bytes 1658880 | tf_op jit(solution)/shard_map/reduce_sum | solution.py:366
  107.5 7.3 %collective-permute-start.11 = (bf16[72,576]{1,0:T(8,128)(2,1)S(1)}, bf16[72,576]{1,0:T(8,128)(2,1)S(1)}, u32[]{:S(2)}, u32[]{:S(2)}) collective-permute-start(bf16[72,576]{1,0:T(8,128)(2,1)S(1)} %get-tuple-element.23), channel_id=1, source_target_pairs={{8,0},{0,8},{9,1},{1,9},{10,2},{2,10},{11,3},{3,11},{12,4},{4,12},... | collective-permute-start | bytes 248840 | tf_op jit(solution)/shard_map/ppermute | solution.py:36
  114.8 0.9 collective-permute-done.11.other
  115.7 1.8 %shares.1 = bf16[8,2,72,576]{3,2,1,0:T(8,128)(2,1)} custom-call(s32[3]{0:T(128)S(1)} %pad_add_fusion.place, bf16[72,576]{1,0:T(8,128)(2,1)S(1)} %get-tuple-element.24.own, bf16[72,576]{1,0:T(8,128)(2,1)S(1)} %collective-permute-done.11.other, bf16[4,40,896]{2,1,0:T(8,128)(2,1)S(1)} %pad_maximum_fusion.1.earlier.refs_0_), custom_call_target="tpu_custom_call" | custom-call | tf_op jit(solution)/shard_map/shares/pallas_call | solution.py:57
  117.4 4.6 %all-to-all-start.2 = ((bf16[8,2,72,576]{3,2,1,0:T(8,128)(2,1)}), bf16[8,2,72,576]{3,2,1,0:T(8,128)(2,1)S(1)}, u32[]{:S(2)}, u32[]{:S(2)}) async-start(bf16[8,2,72,576]{3,2,1,0:T(8,128)(2,1)} %shares.1), calls=%async_computation.2 | async-start | bytes 2949120 | tf_op jit(solution)/shard_map/all_to_all | solution.py:44
  122.1 0.6 collective-permute-start.21
  122.8 0.8 collective-permute-start.23
  123.5 6.0 %collective-permute-start.24 = (bf16[4,40,896]{2,1,0:T(8,128)(2,1)S(1)}, bf16[4,40,896]{2,1,0:T(8,128)(2,1)S(1)}, u32[]{:S(2)}, u32[]{:S(2)}) collective-permute-start(bf16[4,40,896]{2,1,0:T(8,128)(2,1)S(1)} %pad_maximum_fusion.1.earlier.refs_0_), channel_id=1, source_target_pairs={{8,0},{0,8},{9,1},{1,9},{10,2},{2,10},{11,3},{3,11},{12,4},{4,12},... | collective-permute-start | bytes 860168 | tf_op jit(solution)/shard_map/ppermute | solution.py:36
  129.5 7.3 %collective-permute-start.25 = (bf16[4,40,896]{2,1,0:T(8,128)(2,1)S(1)}, bf16[4,40,896]{2,1,0:T(8,128)(2,1)S(1)}, u32[]{:S(2)}, u32[]{:S(2)}) collective-permute-start(bf16[4,40,896]{2,1,0:T(8,128)(2,1)S(1)} %collective-permute-done.21.refs_1_), channel_id=1, source_target_pairs={{8,0},{0,8},{9,1},{1,9},{10,2},{2,10},{11,3},{3,11},{12,4},{4,12},... | collective-permute-start | bytes 860168 | tf_op jit(solution)/shard_map/ppermute | solution.py:36
  136.9 2.9 %collective-permute-start.27 = (bf16[4,40,896]{2,1,0:T(8,128)(2,1)S(1)}, bf16[4,40,896]{2,1,0:T(8,128)(2,1)S(1)}, u32[]{:S(2)}, u32[]{:S(2)}) collective-permute-start(bf16[4,40,896]{2,1,0:T(8,128)(2,1)S(1)} %collective-permute-done.23.refs_3_), channel_id=1, source_target_pairs={{8,0},{0,8},{9,1},{1,9},{10,2},{2,10},{11,3},{3,11},{12,4},{4,12},... | collective-permute-start | bytes 860168 | tf_op jit(solution)/shard_map/ppermute | solution.py:36
  140.5 0.5 collective-permute-done.27.refs_7_
  141.0 0.7 copy-done.6
  141.7 1.0 copy-done.7
  142.7 6.8 %corrected.1 = f32[576,896]{1,0:T(8,128)} custom-call(s32[3]{0:T(128)S(1)} %pad_add_fusion.place, f32[1]{0:T(128)S(6)} %copy.8.damping, bf16[8,2,72,576]{3,2,1,0:T(8,128)(2,1)S(1)} %all-to-all-done.2.acts, bf16[4,40,896]{2,1,0:T(8,128)(2,1)S(1)} %pad_maximum_fusion.1.earlier.refs_0_, bf16[4,40,896]{2,1,0:T(8,128)(2,1)S(1)} %collective-permute-done.21.refs_1_, ...), custom_call_target="tpu_custom_call" | custom-call | tf_op jit(solution)/shard_map/corrected/pallas_call | solution.py:300
  (45 shorter events, 1.3 us)
Async XLA Ops:
  0.0 58.7 %collective-permute-start.8 = (bf16[576,2304]{1,0:T(8,128)(2,1)}, bf16[576,2304]{1,0:T(8,128)(2,1)}, u32[]{:S(2)}, u32[]{:S(2)}) collective-permute-start(bf16[576,2304]{1,0:T(8,128)(2,1)} %bitcast.44), channel_id=1, source_target_pairs={{8,0},{0,8},{9,1},{1,9},{10,2},{2,10},{11,3},{3,11},{12,4},{4,12},... | collective-permute-start | bytes 7962632 | tf_op jit(solution)/shard_map/ppermute | solution.py:36
  5.0 11.4 %collective-permute-start = (bf16[1,40,2304]{2,1,0:T(8,128)(2,1)S(1)}, bf16[1,40,2304]{2,1,0:T(8,128)(2,1)S(1)}, u32[]{:S(2)}, u32[]{:S(2)}) collective-permute-start(bf16[1,40,2304]{2,1,0:T(8,128)(2,1)S(1)} %maximum_bitcast_fusion.own), channel_id=1, source_target_pairs={{16,0},{32,16},{48,32},{0,48},{17,1},{33,17},{49,33},{1,49},{18,2}... | collective-permute-start | bytes 552968 | tf_op jit(solution)/shard_map/ppermute | solution.py:36
  9.3 8.8 %collective-permute-start.1 = (bf16[1,40,2304]{2,1,0:T(8,128)(2,1)S(1)}, bf16[1,40,2304]{2,1,0:T(8,128)(2,1)S(1)}, u32[]{:S(2)}, u32[]{:S(2)}) collective-permute-start(bf16[1,40,2304]{2,1,0:T(8,128)(2,1)S(1)} %maximum_bitcast_fusion.own), channel_id=1, source_target_pairs={{48,0},{0,16},{16,32},{32,48},{49,1},{1,17},{17,33},{33,49},{50,2}... | collective-permute-start | bytes 552968 | tf_op jit(solution)/shard_map/ppermute | solution.py:36
  9.4 0.8 copy-start.8
  10.2 0.7 copy-start.9
  11.6 1.3 collective-permute-start.2
  18.2 4.4 %collective-permute-start.3 = (bf16[1,40,1152]{2,1,0:T(8,128)(2,1)S(1)}, bf16[1,40,1152]{2,1,0:T(8,128)(2,1)S(1)}, u32[]{:S(2)}, u32[]{:S(2)}) collective-permute-start(bf16[1,40,1152]{2,1,0:T(8,128)(2,1)S(1)} %get-tuple-element.12), channel_id=1, source_target_pairs={{16,0},{32,16},{48,32},{0,48},{17,1},{33,17},{49,33},{1,49},{18,2}... | collective-permute-start | bytes 276488 | tf_op jit(solution)/shard_map/ppermute | solution.py:36
  19.6 5.5 %collective-permute-start.4 = (bf16[1,40,1152]{2,1,0:T(8,128)(2,1)S(1)}, bf16[1,40,1152]{2,1,0:T(8,128)(2,1)S(1)}, u32[]{:S(2)}, u32[]{:S(2)}) collective-permute-start(bf16[1,40,1152]{2,1,0:T(8,128)(2,1)S(1)} %get-tuple-element.13), channel_id=1, source_target_pairs={{48,0},{0,16},{16,32},{32,48},{49,1},{1,17},{17,33},{33,49},{50,2}... | collective-permute-start | bytes 276488 | tf_op jit(solution)/shard_map/ppermute | solution.py:36
  25.9 11.6 %copy-start.3 = (bf16[224,896]{1,0:T(8,128)(2,1)S(1)}, bf16[224,896]{1,0:T(8,128)(2,1)}, u32[]{:S(2)}) copy-start(bf16[224,896]{1,0:T(8,128)(2,1)} %basis_own.1) | copy-start | bytes 1204228
  26.8 18.0 %all-to-all-start = ((bf16[8,2,80,224]{3,2,1,0:T(8,128)(2,1)}), bf16[8,2,80,224]{3,2,1,0:T(8,128)(2,1)S(1)}, u32[]{:S(2)}, u32[]{:S(2)}) async-start(bf16[8,2,80,224]{3,2,1,0:T(8,128)(2,1)} %both.1), calls=%async_computation | async-start | bytes 1310720 | tf_op jit(solution)/shard_map/all_to_all | solution.py:44
  35.0 16.5 %collective-permute-start.5 = (bf16[4,40,2304]{2,1,0:T(8,128)(2,1)S(1)}, bf16[4,40,2304]{2,1,0:T(8,128)(2,1)}, u32[]{:S(2)}, u32[]{:S(2)}) collective-permute-start(bf16[4,40,2304]{2,1,0:T(8,128)(2,1)S(1)} %along.1.earlier.refs_0_), channel_id=1, source_target_pairs={{64,0},{128,64},{192,128},{0,192},{65,1},{129,65},{193,129},{1,193... | collective-permute-start | bytes 2211848 | tf_op jit(solution)/shard_map/ppermute | solution.py:36
  37.5 17.3 %collective-permute-start.6 = (bf16[4,40,2304]{2,1,0:T(8,128)(2,1)S(1)}, bf16[4,40,2304]{2,1,0:T(8,128)(2,1)}, u32[]{:S(2)}, u32[]{:S(2)}) collective-permute-start(bf16[4,40,2304]{2,1,0:T(8,128)(2,1)S(1)} %along.1.earlier.refs_0_), channel_id=1, source_target_pairs={{192,0},{0,64},{64,128},{128,192},{193,1},{1,65},{65,129},{129,193... | collective-permute-start | bytes 2211848 | tf_op jit(solution)/shard_map/ppermute | solution.py:36
  37.5 3.4 %collective-permute-start.7 = (bf16[224,896]{1,0:T(8,128)(2,1)S(1)}, bf16[224,896]{1,0:T(8,128)(2,1)S(1)}, u32[]{:S(2)}, u32[]{:S(2)}) collective-permute-start(bf16[224,896]{1,0:T(8,128)(2,1)S(1)} %copy-done.3), channel_id=1, source_target_pairs={{8,0},{0,8},{9,1},{1,9},{10,2},{2,10},{11,3},{3,11},{12,4},{4,12},... | collective-permute-start | bytes 1204232 | tf_op jit(solution)/shard_map/ppermute | solution.py:36
  40.9 0.8 copy-start.4
  44.8 0.8 copy-start.1
  45.6 1.1 copy-start.2
  46.7 1.0 copy-start.5
  49.1 9.6 %copy-start = (bf16[2304,576]{0,1:T(8,128)(2,1)S(1)}, bf16[2304,576]{0,1:T(8,128)(2,1)}, u32[]{:S(2)}) copy-start(bf16[2304,576]{0,1:T(8,128)(2,1)} %param.11) | copy-start | bytes 7962628
  55.9 9.2 %collective-permute-start.10 = (bf16[4,40,1152]{2,1,0:T(8,128)(2,1)S(1)}, bf16[4,40,1152]{2,1,0:T(8,128)(2,1)S(1)}, u32[]{:S(2)}, u32[]{:S(2)}) collective-permute-start(bf16[4,40,1152]{2,1,0:T(8,128)(2,1)S(1)} %get-tuple-element.16), channel_id=1, source_target_pairs={{192,0},{0,64},{64,128},{128,192},{193,1},{1,65},{65,129},{129,193... | collective-permute-start | bytes 1105928 | tf_op jit(solution)/shard_map/ppermute | solution.py:36
  56.0 9.1 %collective-permute-start.9 = (bf16[4,40,1152]{2,1,0:T(8,128)(2,1)S(1)}, bf16[4,40,1152]{2,1,0:T(8,128)(2,1)S(1)}, u32[]{:S(2)}, u32[]{:S(2)}) collective-permute-start(bf16[4,40,1152]{2,1,0:T(8,128)(2,1)S(1)} %get-tuple-element.15.earlier), channel_id=1, source_target_pairs={{64,0},{128,64},{192,128},{0,192},{65,1},{129,65},{193,129},{1,193... | collective-permute-start | bytes 1105928 | tf_op jit(solution)/shard_map/ppermute | solution.py:36
  70.4 35.4 %all-to-all-start.1 = ((f16[8,72,1152]{2,1,0:T(8,128)(2,1)}), f16[8,72,1152]{2,1,0:T(8,128)(2,1)}, u32[]{:S(2)}, u32[]{:S(2)}) async-start(f16[8,72,1152]{2,1,0:T(8,128)(2,1)} %pad_maximum_fusion), calls=%async_computation.1 | async-start | bytes 2654208 | tf_op jit(solution)/shard_map/all_to_all | solution.py:44
  75.6 10.2 %collective-permute-start.12 = (f16[4,40,896]{2,1,0:T(8,128)(2,1)S(1)}, f16[4,40,896]{2,1,0:T(8,128)(2,1)S(1)}, u32[]{:S(2)}, u32[]{:S(2)}) collective-permute-start(f16[4,40,896]{2,1,0:T(8,128)(2,1)S(1)} %get-tuple-element.17), channel_id=1, source_target_pairs={{192,0},{0,64},{64,128},{128,192},{193,1},{1,65},{65,129},{129,193... | collective-permute-start | bytes 860168 | tf_op jit(solution)/shard_map/ppermute | solution.py:36
  75.7 10.3 %collective-permute-start.13 = (f16[4,40,896]{2,1,0:T(8,128)(2,1)S(1)}, f16[4,40,896]{2,1,0:T(8,128)(2,1)}, u32[]{:S(2)}, u32[]{:S(2)}) collective-permute-start(f16[4,40,896]{2,1,0:T(8,128)(2,1)S(1)} %get-tuple-element.19), channel_id=1, source_target_pairs={{128,0},{192,64},{0,128},{64,192},{129,1},{193,65},{1,129},{65,193... | collective-permute-start | bytes 860168 | tf_op jit(solution)/shard_map/ppermute | solution.py:36
  78.0 10.8 %collective-permute-start.14 = (f16[4,40,896]{2,1,0:T(8,128)(2,1)S(1)}, f16[4,40,896]{2,1,0:T(8,128)(2,1)}, u32[]{:S(2)}, u32[]{:S(2)}) collective-permute-start(f16[4,40,896]{2,1,0:T(8,128)(2,1)S(1)} %get-tuple-element.18), channel_id=1, source_target_pairs={{64,0},{128,64},{192,128},{0,192},{65,1},{129,65},{193,129},{1,193... | collective-permute-start | bytes 860168 | tf_op jit(solution)/shard_map/ppermute | solution.py:36
  90.1 5.4 %collective-permute-start.15 = (f16[40,896]{1,0:T(8,128)(2,1)S(1)}, f16[40,896]{1,0:T(8,128)(2,1)S(1)}, u32[]{:S(2)}, u32[]{:S(2)}) collective-permute-start(f16[40,896]{1,0:T(8,128)(2,1)S(1)} %get-tuple-element.20), channel_id=1, source_target_pairs={{48,0},{0,16},{16,32},{32,48},{49,1},{1,17},{17,33},{33,49},{50,2}... | collective-permute-start | bytes 215048 | tf_op jit(solution)/shard_map/ppermute | solution.py:36
  90.2 7.7 %collective-permute-start.16 = (f16[40,896]{1,0:T(8,128)(2,1)S(1)}, f16[40,896]{1,0:T(8,128)(2,1)S(1)}, u32[]{:S(2)}, u32[]{:S(2)}) collective-permute-start(f16[40,896]{1,0:T(8,128)(2,1)S(1)} %get-tuple-element.22), channel_id=1, source_target_pairs={{32,0},{48,16},{0,32},{16,48},{33,1},{49,17},{1,33},{17,49},{34,2}... | collective-permute-start | bytes 215048 | tf_op jit(solution)/shard_map/ppermute | solution.py:36
  94.7 4.3 %collective-permute-start.17 = (f16[40,896]{1,0:T(8,128)(2,1)S(1)}, f16[40,896]{1,0:T(8,128)(2,1)S(1)}, u32[]{:S(2)}, u32[]{:S(2)}) collective-permute-start(f16[40,896]{1,0:T(8,128)(2,1)S(1)} %get-tuple-element.21), channel_id=1, source_target_pairs={{16,0},{32,16},{48,32},{0,48},{17,1},{33,17},{49,33},{1,49},{18,2}... | collective-permute-start | bytes 215048 | tf_op jit(solution)/shard_map/ppermute | solution.py:36
  99.0 15.7 %collective-permute-start.18 = (bf16[40,896]{1,0:T(8,128)(2,1)S(1)}, bf16[40,896]{1,0:T(8,128)(2,1)S(1)}, u32[]{:S(2)}, u32[]{:S(2)}) collective-permute-start(bf16[40,896]{1,0:T(8,128)(2,1)S(1)} %fusion.7), channel_id=1, source_target_pairs={{16,0},{32,16},{48,32},{0,48},{17,1},{33,17},{49,33},{1,49},{18,2}... | collective-permute-start | bytes 215048 | tf_op jit(solution)/shard_map/ppermute | solution.py:36
  101.1 13.6 %collective-permute-start.19 = (bf16[40,896]{1,0:T(8,128)(2,1)S(1)}, bf16[40,896]{1,0:T(8,128)(2,1)S(1)}, u32[]{:S(2)}, u32[]{:S(2)}) collective-permute-start(bf16[40,896]{1,0:T(8,128)(2,1)S(1)} %fusion.7), channel_id=1, source_target_pairs={{32,0},{48,16},{0,32},{16,48},{33,1},{49,17},{1,33},{17,49},{34,2}... | collective-permute-start | bytes 215048 | tf_op jit(solution)/shard_map/ppermute | solution.py:36
  105.2 9.5 %collective-permute-start.20 = (bf16[40,896]{1,0:T(8,128)(2,1)S(1)}, bf16[40,896]{1,0:T(8,128)(2,1)S(1)}, u32[]{:S(2)}, u32[]{:S(2)}) collective-permute-start(bf16[40,896]{1,0:T(8,128)(2,1)S(1)} %fusion.7), channel_id=1, source_target_pairs={{48,0},{0,16},{16,32},{32,48},{49,1},{1,17},{17,33},{33,49},{50,2}... | collective-permute-start | bytes 215048 | tf_op jit(solution)/shard_map/ppermute | solution.py:36
  107.5 8.2 %collective-permute-start.11 = (bf16[72,576]{1,0:T(8,128)(2,1)S(1)}, bf16[72,576]{1,0:T(8,128)(2,1)S(1)}, u32[]{:S(2)}, u32[]{:S(2)}) collective-permute-start(bf16[72,576]{1,0:T(8,128)(2,1)S(1)} %get-tuple-element.23), channel_id=1, source_target_pairs={{8,0},{0,8},{9,1},{1,9},{10,2},{2,10},{11,3},{3,11},{12,4},{4,12},... | collective-permute-start | bytes 248840 | tf_op jit(solution)/shard_map/ppermute | solution.py:36
  117.4 24.3 %all-to-all-start.2 = ((bf16[8,2,72,576]{3,2,1,0:T(8,128)(2,1)}), bf16[8,2,72,576]{3,2,1,0:T(8,128)(2,1)S(1)}, u32[]{:S(2)}, u32[]{:S(2)}) async-start(bf16[8,2,72,576]{3,2,1,0:T(8,128)(2,1)} %shares.1), calls=%async_computation.2 | async-start | bytes 2949120 | tf_op jit(solution)/shard_map/all_to_all | solution.py:44
  122.1 7.5 %collective-permute-start.21 = (bf16[4,40,896]{2,1,0:T(8,128)(2,1)S(1)}, bf16[4,40,896]{2,1,0:T(8,128)(2,1)S(1)}, u32[]{:S(2)}, u32[]{:S(2)}) collective-permute-start(bf16[4,40,896]{2,1,0:T(8,128)(2,1)S(1)} %pad_maximum_fusion.1.earlier.refs_0_), channel_id=1, source_target_pairs={{64,0},{128,64},{192,128},{0,192},{65,1},{129,65},{193,129},{1,193... | collective-permute-start | bytes 860168 | tf_op jit(solution)/shard_map/ppermute | solution.py:36
  122.7 14.2 %collective-permute-start.22 = (bf16[4,40,896]{2,1,0:T(8,128)(2,1)S(1)}, bf16[4,40,896]{2,1,0:T(8,128)(2,1)S(1)}, u32[]{:S(2)}, u32[]{:S(2)}) collective-permute-start(bf16[4,40,896]{2,1,0:T(8,128)(2,1)S(1)} %pad_maximum_fusion.1.earlier.refs_0_), channel_id=1, source_target_pairs={{128,0},{192,64},{0,128},{64,192},{129,1},{193,65},{1,129},{65,193... | collective-permute-start | bytes 860168 | tf_op jit(solution)/shard_map/ppermute | solution.py:36
  122.8 14.1 %collective-permute-start.23 = (bf16[4,40,896]{2,1,0:T(8,128)(2,1)S(1)}, bf16[4,40,896]{2,1,0:T(8,128)(2,1)S(1)}, u32[]{:S(2)}, u32[]{:S(2)}) collective-permute-start(bf16[4,40,896]{2,1,0:T(8,128)(2,1)S(1)} %pad_maximum_fusion.1.earlier.refs_0_), channel_id=1, source_target_pairs={{192,0},{0,64},{64,128},{128,192},{193,1},{1,65},{65,129},{129,193... | collective-permute-start | bytes 860168 | tf_op jit(solution)/shard_map/ppermute | solution.py:36
  123.5 16.9 %collective-permute-start.24 = (bf16[4,40,896]{2,1,0:T(8,128)(2,1)S(1)}, bf16[4,40,896]{2,1,0:T(8,128)(2,1)S(1)}, u32[]{:S(2)}, u32[]{:S(2)}) collective-permute-start(bf16[4,40,896]{2,1,0:T(8,128)(2,1)S(1)} %pad_maximum_fusion.1.earlier.refs_0_), channel_id=1, source_target_pairs={{8,0},{0,8},{9,1},{1,9},{10,2},{2,10},{11,3},{3,11},{12,4},{4,12},... | collective-permute-start | bytes 860168 | tf_op jit(solution)/shard_map/ppermute | solution.py:36
  129.5 10.9 %collective-permute-start.25 = (bf16[4,40,896]{2,1,0:T(8,128)(2,1)S(1)}, bf16[4,40,896]{2,1,0:T(8,128)(2,1)S(1)}, u32[]{:S(2)}, u32[]{:S(2)}) collective-permute-start(bf16[4,40,896]{2,1,0:T(8,128)(2,1)S(1)} %collective-permute-done.21.refs_1_), channel_id=1, source_target_pairs={{8,0},{0,8},{9,1},{1,9},{10,2},{2,10},{11,3},{3,11},{12,4},{4,12},... | collective-permute-start | bytes 860168 | tf_op jit(solution)/shard_map/ppermute | solution.py:36
  136.9 3.6 %collective-permute-start.26 = (bf16[4,40,896]{2,1,0:T(8,128)(2,1)S(1)}, bf16[4,40,896]{2,1,0:T(8,128)(2,1)S(1)}, u32[]{:S(2)}, u32[]{:S(2)}) collective-permute-start(bf16[4,40,896]{2,1,0:T(8,128)(2,1)S(1)} %collective-permute-done.22.refs_2_), channel_id=1, source_target_pairs={{8,0},{0,8},{9,1},{1,9},{10,2},{2,10},{11,3},{3,11},{12,4},{4,12},... | collective-permute-start | bytes 860168 | tf_op jit(solution)/shard_map/ppermute | solution.py:36
  136.9 4.1 %collective-permute-start.27 = (bf16[4,40,896]{2,1,0:T(8,128)(2,1)S(1)}, bf16[4,40,896]{2,1,0:T(8,128)(2,1)S(1)}, u32[]{:S(2)}, u32[]{:S(2)}) collective-permute-start(bf16[4,40,896]{2,1,0:T(8,128)(2,1)S(1)} %collective-permute-done.23.refs_3_), channel_id=1, source_target_pairs={{8,0},{0,8},{9,1},{1,9},{10,2},{2,10},{11,3},{3,11},{12,4},{4,12},... | collective-permute-start | bytes 860168 | tf_op jit(solution)/shard_map/ppermute | solution.py:36
  141.0 0.7 copy-start.6
  141.7 1.0 copy-start.7

commit v3 on v2

--- a/solution.py
+++ b/solution.py
@@ -266,7 +266,7 @@
     grads_own, grads_other, out = refs[:4], refs[4:8], refs[8]
     core, x, zh = place[0], place[1], place[2]
     width, height = out.shape
-    tile = 192
+    tile = 256
 
     for left in range(0, width, tile):
         cols = slice(left, min(left + tile, width))

time: 150 us -> 150 us (level)
  no operation moved by 1% of the time
where the time goes in v3:
time: 150 us; the launch traced here: 149 us
  starting transfers between devices  74.6 us (50%)
  waiting for transfers between devices  36.9 us (25%)
  Pallas kernels  23.4 us (16%)
  local copies, waits for them, and re-layouts  7.29 us (5%)
  other arithmetic  6.45 us (4%)
    ppermute x28, starting transfers between devices, from_ahead(): lax.ppermute(value, axis, [((i + by) % size, i) for i in range(size)])  56.9 us
    ppermute x28, waiting for transfers between devices, from_ahead(): lax.ppermute(value, axis, [((i + by) % size, i) for i in range(size)])  33.7 us
    all_to_all x3, starting transfers between devices, exchanged(): return lax.all_to_all(blocks, axis, 0, 0, tiled=True)  17.7 us
    pallas_call x2, Pallas kernels, rotated_in(): pl.pallas_call(functools.partial(rotate_in_kernel, count), out_shape=jax....  9.93 us
    unnamed x20, local copies, waits for them, and re-layouts  6.88 us
    pallas_call x1, Pallas kernels, corrected(): pl.pallas_call(final_kernel, out_shape=jax.ShapeDtypeStruct(shape, F32),...  6.85 us
    all_to_all x3, waiting for transfers between devices, exchanged(): return lax.all_to_all(blocks, axis, 0, 0, tiled=True)  3.19 us
  transfers between devices with their start and end apart: 31, of which 17 were waited for; matrix products, arithmetic and copies ran while one was open for 4% of the time, Pallas kernels for 7%

profile of v3, /device:TPU:1, one launch (start us, length us, event | category | flops | bytes accessed | tf_op | source)
XLA Modules:
  0.0 149.5 jit_solution(11389181553686892976)
XLA Ops:
  0.0 3.2 %collective-permute-start.8 = (bf16[576,2304]{1,0:T(8,128)(2,1)}, bf16[576,2304]{1,0:T(8,128)(2,1)}, u32[]{:S(2)}, u32[]{:S(2)}) collective-permute-start(bf16[576,2304]{1,0:T(8,128)(2,1)} %bitcast.44), channel_id=1, source_target_pairs={{8,0},{0,8},{9,1},{1,9},{10,2},{2,10},{11,3},{3,11},{12,4},{4,12},... | collective-permute-start | bytes 7962632 | tf_op jit(solution)/shard_map/ppermute | solution.py:36
  3.2 0.8 pad_select_fusion
  4.0 0.9 maximum_bitcast_fusion.own
  5.0 4.4 %collective-permute-start = (bf16[1,40,2304]{2,1,0:T(8,128)(2,1)S(1)}, bf16[1,40,2304]{2,1,0:T(8,128)(2,1)S(1)}, u32[]{:S(2)}, u32[]{:S(2)}) collective-permute-start(bf16[1,40,2304]{2,1,0:T(8,128)(2,1)S(1)} %maximum_bitcast_fusion.own), channel_id=1, source_target_pairs={{16,0},{32,16},{48,32},{0,48},{17,1},{33,17},{49,33},{1,49},{18,2}... | collective-permute-start | bytes 552968 | tf_op jit(solution)/shard_map/ppermute | solution.py:36
  9.4 0.8 copy-done.8
  10.2 0.7 copy-done.9
  10.9 0.6 token_halves.1
  11.6 0.4 collective-permute-start.2
  11.9 0.9 collective-permute-done.2.earlier.other
  12.9 3.5 %collective-permute-done.ahead = bf16[1,40,2304]{2,1,0:T(8,128)(2,1)S(1)} collective-permute-done((bf16[1,40,2304]{2,1,0:T(8,128)(2,1)S(1)}, bf16[1,40,2304]{2,1,0:T(8,128)(2,1)S(1)}, u32[]{:S(2)}, u32[]{:S(2)}) %collective-permute-start) | collective-permute-done | bytes 184352 | tf_op jit(solution)/shard_map/ppermute | solution.py:36
  16.3 1.8 %collective-permute-done.1.back = bf16[1,40,2304]{2,1,0:T(8,128)(2,1)S(1)} collective-permute-done((bf16[1,40,2304]{2,1,0:T(8,128)(2,1)S(1)}, bf16[1,40,2304]{2,1,0:T(8,128)(2,1)S(1)}, u32[]{:S(2)}, u32[]{:S(2)}) %collective-permute-start.1) | collective-permute-done | bytes 184352 | tf_op jit(solution)/shard_map/ppermute | solution.py:36
  18.2 1.4 collective-permute-start.3
  19.6 1.0 collective-permute-start.4
  20.6 1.9 %collective-permute-done.3.left = bf16[1,40,1152]{2,1,0:T(8,128)(2,1)S(1)} collective-permute-done((bf16[1,40,1152]{2,1,0:T(8,128)(2,1)S(1)}, bf16[1,40,1152]{2,1,0:T(8,128)(2,1)S(1)}, u32[]{:S(2)}, u32[]{:S(2)}) %collective-permute-start.3) | collective-permute-done | bytes 92192 | tf_op jit(solution)/shard_map/ppermute | solution.py:36
  22.6 2.6 %collective-permute-done.4.right = bf16[1,40,1152]{2,1,0:T(8,128)(2,1)S(1)} collective-permute-done((bf16[1,40,1152]{2,1,0:T(8,128)(2,1)S(1)}, bf16[1,40,1152]{2,1,0:T(8,128)(2,1)S(1)}, u32[]{:S(2)}, u32[]{:S(2)}) %collective-permute-start.4) | collective-permute-done | bytes 92192 | tf_op jit(solution)/shard_map/ppermute | solution.py:36
  25.1 0.8 along.1.earlier.refs_0_
  25.9 0.9 both.1
  26.8 8.2 %all-to-all-start = ((bf16[8,2,80,224]{3,2,1,0:T(8,128)(2,1)}), bf16[8,2,80,224]{3,2,1,0:T(8,128)(2,1)S(1)}, u32[]{:S(2)}, u32[]{:S(2)}) async-start(bf16[8,2,80,224]{3,2,1,0:T(8,128)(2,1)} %both.1), calls=%async_computation | async-start | bytes 1310720 | tf_op jit(solution)/shard_map/all_to_all | solution.py:44
  35.0 2.5 %collective-permute-start.5 = (bf16[4,40,2304]{2,1,0:T(8,128)(2,1)S(1)}, bf16[4,40,2304]{2,1,0:T(8,128)(2,1)}, u32[]{:S(2)}, u32[]{:S(2)}) collective-permute-start(bf16[4,40,2304]{2,1,0:T(8,128)(2,1)S(1)} %along.1.earlier.refs_0_), channel_id=1, source_target_pairs={{64,0},{128,64},{192,128},{0,192},{65,1},{129,65},{193,129},{1,193... | collective-permute-start | bytes 2211848 | tf_op jit(solution)/shard_map/ppermute | solution.py:36
  37.5 2.0 %collective-permute-start.7 = (bf16[224,896]{1,0:T(8,128)(2,1)S(1)}, bf16[224,896]{1,0:T(8,128)(2,1)S(1)}, u32[]{:S(2)}, u32[]{:S(2)}) collective-permute-start(bf16[224,896]{1,0:T(8,128)(2,1)S(1)} %copy-done.3), channel_id=1, source_target_pairs={{8,0},{0,8},{9,1},{1,9},{10,2},{2,10},{11,3},{3,11},{12,4},{4,12},... | collective-permute-start | bytes 1204232 | tf_op jit(solution)/shard_map/ppermute | solution.py:36
  39.5 1.4 collective-permute-done.7.basis_other
  40.9 0.8 copy-done.4
  41.6 3.2 %all-to-all-done.tokens = bf16[8,2,80,224]{3,2,1,0:T(8,128)(2,1)S(1)} async-done(((bf16[8,2,80,224]{3,2,1,0:T(8,128)(2,1)}), bf16[8,2,80,224]{3,2,1,0:T(8,128)(2,1)S(1)}, u32[]{:S(2)}, u32[]{:S(2)}) %all-to-all-start) | async-done | bytes 573472 | tf_op jit(solution)/shard_map/all_to_all | solution.py:44
  44.8 0.8 copy-done.1
  45.7 1.1 copy-done.2
  46.7 1.0 copy-done.5
  47.7 1.4 rotated_out.1.earlier
  49.1 2.4 %collective-permute-done.5.ahead.refs_1_ = bf16[4,40,2304]{2,1,0:T(8,128)(2,1)} collective-permute-done((bf16[4,40,2304]{2,1,0:T(8,128)(2,1)S(1)}, bf16[4,40,2304]{2,1,0:T(8,128)(2,1)}, u32[]{:S(2)}, u32[]{:S(2)}) %collective-permute-start.5) | collective-permute-done | bytes 737312 | tf_op jit(solution)/shard_map/ppermute | solution.py:36
  51.6 3.2 %collective-permute-done.6.back.refs_2_ = bf16[4,40,2304]{2,1,0:T(8,128)(2,1)} collective-permute-done((bf16[4,40,2304]{2,1,0:T(8,128)(2,1)S(1)}, bf16[4,40,2304]{2,1,0:T(8,128)(2,1)}, u32[]{:S(2)}, u32[]{:S(2)}) %collective-permute-start.6) | collective-permute-done | bytes 737312 | tf_op jit(solution)/shard_map/ppermute | solution.py:36
  54.8 1.1 sides.3
  56.0 2.7 %collective-permute-start.9 = (bf16[4,40,1152]{2,1,0:T(8,128)(2,1)S(1)}, bf16[4,40,1152]{2,1,0:T(8,128)(2,1)S(1)}, u32[]{:S(2)}, u32[]{:S(2)}) collective-permute-start(bf16[4,40,1152]{2,1,0:T(8,128)(2,1)S(1)} %get-tuple-element.15.earlier), channel_id=1, source_target_pairs={{64,0},{128,64},{192,128},{0,192},{65,1},{129,65},{193,129},{1,193... | collective-permute-start | bytes 1105928 | tf_op jit(solution)/shard_map/ppermute | solution.py:36
  58.7 6.1 %rotated_in.2.earlier = f32[6,72,1152]{2,1,0:T(8,128)S(1)} custom-call(s32[3]{0:T(128)S(1)} %pad_add_fusion.place, bf16[4,40,1152]{2,1,0:T(8,128)(2,1)S(1)} %get-tuple-element.15.earlier, bf16[4,40,2304]{2,1,0:T(8,128)(2,1)S(1)} %along.1.earlier.refs_0_, bf16[4,40,2304]{2,1,0:T(8,128)(2,1)} %collective-permute-done.5.ahead.refs_1_, ...), custom_call_target="tpu_custom_call" | custom-call | tf_op jit(solution)/shard_map/rotated_in/pallas_call | solution.py:248
  65.1 3.8 %rotated_in.3 = f32[2,72,1152]{2,1,0:T(8,128)S(1)} custom-call(s32[3]{0:T(128)S(1)} %pad_add_fusion.place, f32[6,72,1152]{2,1,0:T(8,128)S(1)} %rotated_in.2.earlier, bf16[4,40,1152]{2,1,0:T(8,128)(2,1)S(1)} %collective-permute-done.9.refs_0_, bf16[4,40,1152]{2,1,0:T(8,128)(2,1)S(1)} %collective-permute-done.10.refs_1_, bf16[576,2304]{1,0:T(8,128)(2,1)S(1)} %bitcast.46, ...), custom_call_target="tpu_custom_call" | custom-call | tf_op jit(solution)/shard_map/rotated_in/pallas_call | solution.py:248
  69.0 1.4 pad_maximum_fusion
  70.4 4.9 %all-to-all-start.1 = ((f16[8,72,1152]{2,1,0:T(8,128)(2,1)}), f16[8,72,1152]{2,1,0:T(8,128)(2,1)}, u32[]{:S(2)}, u32[]{:S(2)}) async-start(f16[8,72,1152]{2,1,0:T(8,128)(2,1)} %pad_maximum_fusion), calls=%async_computation.1 | async-start | bytes 2654208 | tf_op jit(solution)/shard_map/all_to_all | solution.py:44
  75.3 0.1 convert.14
  75.4 0.1 slice_bitcast_fusion.3
  75.7 2.3 %collective-permute-start.13 = (f16[4,40,896]{2,1,0:T(8,128)(2,1)S(1)}, f16[4,40,896]{2,1,0:T(8,128)(2,1)}, u32[]{:S(2)}, u32[]{:S(2)}) collective-permute-start(f16[4,40,896]{2,1,0:T(8,128)(2,1)S(1)} %get-tuple-element.19), channel_id=1, source_target_pairs={{128,0},{192,64},{0,128},{64,192},{129,1},{193,65},{1,129},{65,193... | collective-permute-start | bytes 860168 | tf_op jit(solution)/shard_map/ppermute | solution.py:36
  78.0 0.4 collective-permute-start.14
  78.3 7.4 %collective-permute-done.12 = f16[4,40,896]{2,1,0:T(8,128)(2,1)S(1)} collective-permute-done((f16[4,40,896]{2,1,0:T(8,128)(2,1)S(1)}, f16[4,40,896]{2,1,0:T(8,128)(2,1)S(1)}, u32[]{:S(2)}, u32[]{:S(2)}) %collective-permute-start.12) | collective-permute-done | bytes 286752 | tf_op jit(solution)/shard_map/ppermute | solution.py:36
  85.8 0.2 collective-permute-done.13
  86.0 2.8 %collective-permute-done.14 = f16[4,40,896]{2,1,0:T(8,128)(2,1)} collective-permute-done((f16[4,40,896]{2,1,0:T(8,128)(2,1)S(1)}, f16[4,40,896]{2,1,0:T(8,128)(2,1)}, u32[]{:S(2)}, u32[]{:S(2)}) %collective-permute-start.14) | collective-permute-done | bytes 286752 | tf_op jit(solution)/shard_map/ppermute | solution.py:36
  88.8 1.2 fusion.3
  90.2 4.6 %collective-permute-start.16 = (f16[40,896]{1,0:T(8,128)(2,1)S(1)}, f16[40,896]{1,0:T(8,128)(2,1)S(1)}, u32[]{:S(2)}, u32[]{:S(2)}) collective-permute-start(f16[40,896]{1,0:T(8,128)(2,1)S(1)} %get-tuple-element.22), channel_id=1, source_target_pairs={{32,0},{48,16},{0,32},{16,48},{33,1},{49,17},{1,33},{17,49},{34,2}... | collective-permute-start | bytes 215048 | tf_op jit(solution)/shard_map/ppermute | solution.py:36
  94.8 0.6 collective-permute-done.15
  95.4 2.4 %collective-permute-done.16 = f16[40,896]{1,0:T(8,128)(2,1)S(1)} collective-permute-done((f16[40,896]{1,0:T(8,128)(2,1)S(1)}, f16[40,896]{1,0:T(8,128)(2,1)S(1)}, u32[]{:S(2)}, u32[]{:S(2)}) %collective-permute-start.16) | collective-permute-done | bytes 71712 | tf_op jit(solution)/shard_map/ppermute | solution.py:36
  97.8 1.1 collective-permute-done.17
  99.0 2.1 %collective-permute-start.18 = (bf16[40,896]{1,0:T(8,128)(2,1)S(1)}, bf16[40,896]{1,0:T(8,128)(2,1)S(1)}, u32[]{:S(2)}, u32[]{:S(2)}) collective-permute-start(bf16[40,896]{1,0:T(8,128)(2,1)S(1)} %fusion.7), channel_id=1, source_target_pairs={{16,0},{32,16},{48,32},{0,48},{17,1},{33,17},{49,33},{1,49},{18,2}... | collective-permute-start | bytes 215048 | tf_op jit(solution)/shard_map/ppermute | solution.py:36
  101.1 4.1 %collective-permute-start.19 = (bf16[40,896]{1,0:T(8,128)(2,1)S(1)}, bf16[40,896]{1,0:T(8,128)(2,1)S(1)}, u32[]{:S(2)}, u32[]{:S(2)}) collective-permute-start(bf16[40,896]{1,0:T(8,128)(2,1)S(1)} %fusion.7), channel_id=1, source_target_pairs={{32,0},{48,16},{0,32},{16,48},{33,1},{49,17},{1,33},{17,49},{34,2}... | collective-permute-start | bytes 215048 | tf_op jit(solution)/shard_map/ppermute | solution.py:36
  105.2 0.6 collective-permute-start.20
  105.8 1.5 %convert_reduce_fusion = f32[72,1152]{1,0:T(8,128)S(1)} fusion(f16[8,72,1152]{2,1,0:T(8,128)(2,1)} %all-to-all-done.1), kind=kLoop, calls=%fused_computation | loop fusion | flops 1244160 | bytes 1658880 | tf_op jit(solution)/shard_map/reduce_sum | solution.py:366
  107.5 7.3 %collective-permute-start.11 = (bf16[72,576]{1,0:T(8,128)(2,1)S(1)}, bf16[72,576]{1,0:T(8,128)(2,1)S(1)}, u32[]{:S(2)}, u32[]{:S(2)}) collective-permute-start(bf16[72,576]{1,0:T(8,128)(2,1)S(1)} %get-tuple-element.23), channel_id=1, source_target_pairs={{8,0},{0,8},{9,1},{1,9},{10,2},{2,10},{11,3},{3,11},{12,4},{4,12},... | collective-permute-start | bytes 248840 | tf_op jit(solution)/shard_map/ppermute | solution.py:36
  114.8 0.9 collective-permute-done.11.other
  115.7 1.8 %shares.1 = bf16[8,2,72,576]{3,2,1,0:T(8,128)(2,1)} custom-call(s32[3]{0:T(128)S(1)} %pad_add_fusion.place, bf16[72,576]{1,0:T(8,128)(2,1)S(1)} %get-tuple-element.24.own, bf16[72,576]{1,0:T(8,128)(2,1)S(1)} %collective-permute-done.11.other, bf16[4,40,896]{2,1,0:T(8,128)(2,1)S(1)} %pad_maximum_fusion.1.earlier.refs_0_), custom_call_target="tpu_custom_call" | custom-call | tf_op jit(solution)/shard_map/shares/pallas_call | solution.py:57
  117.4 4.6 %all-to-all-start.2 = ((bf16[8,2,72,576]{3,2,1,0:T(8,128)(2,1)}), bf16[8,2,72,576]{3,2,1,0:T(8,128)(2,1)S(1)}, u32[]{:S(2)}, u32[]{:S(2)}) async-start(bf16[8,2,72,576]{3,2,1,0:T(8,128)(2,1)} %shares.1), calls=%async_computation.2 | async-start | bytes 2949120 | tf_op jit(solution)/shard_map/all_to_all | solution.py:44
  122.1 0.6 collective-permute-start.21
  122.8 0.8 collective-permute-start.23
  123.5 6.0 %collective-permute-start.24 = (bf16[4,40,896]{2,1,0:T(8,128)(2,1)S(1)}, bf16[4,40,896]{2,1,0:T(8,128)(2,1)S(1)}, u32[]{:S(2)}, u32[]{:S(2)}) collective-permute-start(bf16[4,40,896]{2,1,0:T(8,128)(2,1)S(1)} %pad_maximum_fusion.1.earlier.refs_0_), channel_id=1, source_target_pairs={{8,0},{0,8},{9,1},{1,9},{10,2},{2,10},{11,3},{3,11},{12,4},{4,12},... | collective-permute-start | bytes 860168 | tf_op jit(solution)/shard_map/ppermute | solution.py:36
  129.5 7.3 %collective-permute-start.25 = (bf16[4,40,896]{2,1,0:T(8,128)(2,1)S(1)}, bf16[4,40,896]{2,1,0:T(8,128)(2,1)S(1)}, u32[]{:S(2)}, u32[]{:S(2)}) collective-permute-start(bf16[4,40,896]{2,1,0:T(8,128)(2,1)S(1)} %collective-permute-done.21.refs_1_), channel_id=1, source_target_pairs={{8,0},{0,8},{9,1},{1,9},{10,2},{2,10},{11,3},{3,11},{12,4},{4,12},... | collective-permute-start | bytes 860168 | tf_op jit(solution)/shard_map/ppermute | solution.py:36
  136.9 2.9 %collective-permute-start.27 = (bf16[4,40,896]{2,1,0:T(8,128)(2,1)S(1)}, bf16[4,40,896]{2,1,0:T(8,128)(2,1)S(1)}, u32[]{:S(2)}, u32[]{:S(2)}) collective-permute-start(bf16[4,40,896]{2,1,0:T(8,128)(2,1)S(1)} %collective-permute-done.23.refs_3_), channel_id=1, source_target_pairs={{8,0},{0,8},{9,1},{1,9},{10,2},{2,10},{11,3},{3,11},{12,4},{4,12},... | collective-permute-start | bytes 860168 | tf_op jit(solution)/shard_map/ppermute | solution.py:36
  140.5 0.5 collective-permute-done.27.refs_7_
  141.0 0.7 copy-done.6
  141.7 1.0 copy-done.7
  142.7 6.8 %corrected.1 = f32[576,896]{1,0:T(8,128)} custom-call(s32[3]{0:T(128)S(1)} %pad_add_fusion.place, f32[1]{0:T(128)S(6)} %copy.8.damping, bf16[8,2,72,576]{3,2,1,0:T(8,128)(2,1)S(1)} %all-to-all-done.2.acts, bf16[4,40,896]{2,1,0:T(8,128)(2,1)S(1)} %pad_maximum_fusion.1.earlier.refs_0_, bf16[4,40,896]{2,1,0:T(8,128)(2,1)S(1)} %collective-permute-done.21.refs_1_, ...), custom_call_target="tpu_custom_call" | custom-call | tf_op jit(solution)/shard_map/corrected/pallas_call | solution.py:300
  (45 shorter events, 1.3 us)
Async XLA Ops:
  0.0 58.7 %collective-permute-start.8 = (bf16[576,2304]{1,0:T(8,128)(2,1)}, bf16[576,2304]{1,0:T(8,128)(2,1)}, u32[]{:S(2)}, u32[]{:S(2)}) collective-permute-start(bf16[576,2304]{1,0:T(8,128)(2,1)} %bitcast.44), channel_id=1, source_target_pairs={{8,0},{0,8},{9,1},{1,9},{10,2},{2,10},{11,3},{3,11},{12,4},{4,12},... | collective-permute-start | bytes 7962632 | tf_op jit(solution)/shard_map/ppermute | solution.py:36
  5.0 11.4 %collective-permute-start = (bf16[1,40,2304]{2,1,0:T(8,128)(2,1)S(1)}, bf16[1,40,2304]{2,1,0:T(8,128)(2,1)S(1)}, u32[]{:S(2)}, u32[]{:S(2)}) collective-permute-start(bf16[1,40,2304]{2,1,0:T(8,128)(2,1)S(1)} %maximum_bitcast_fusion.own), channel_id=1, source_target_pairs={{16,0},{32,16},{48,32},{0,48},{17,1},{33,17},{49,33},{1,49},{18,2}... | collective-permute-start | bytes 552968 | tf_op jit(solution)/shard_map/ppermute | solution.py:36
  9.3 8.8 %collective-permute-start.1 = (bf16[1,40,2304]{2,1,0:T(8,128)(2,1)S(1)}, bf16[1,40,2304]{2,1,0:T(8,128)(2,1)S(1)}, u32[]{:S(2)}, u32[]{:S(2)}) collective-permute-start(bf16[1,40,2304]{2,1,0:T(8,128)(2,1)S(1)} %maximum_bitcast_fusion.own), channel_id=1, source_target_pairs={{48,0},{0,16},{16,32},{32,48},{49,1},{1,17},{17,33},{33,49},{50,2}... | collective-permute-start | bytes 552968 | tf_op jit(solution)/shard_map/ppermute | solution.py:36
  9.4 0.8 copy-start.8
  10.2 0.7 copy-start.9
  11.6 1.3 collective-permute-start.2
  18.2 4.4 %collective-permute-start.3 = (bf16[1,40,1152]{2,1,0:T(8,128)(2,1)S(1)}, bf16[1,40,1152]{2,1,0:T(8,128)(2,1)S(1)}, u32[]{:S(2)}, u32[]{:S(2)}) collective-permute-start(bf16[1,40,1152]{2,1,0:T(8,128)(2,1)S(1)} %get-tuple-element.12), channel_id=1, source_target_pairs={{16,0},{32,16},{48,32},{0,48},{17,1},{33,17},{49,33},{1,49},{18,2}... | collective-permute-start | bytes 276488 | tf_op jit(solution)/shard_map/ppermute | solution.py:36
  19.6 5.5 %collective-permute-start.4 = (bf16[1,40,1152]{2,1,0:T(8,128)(2,1)S(1)}, bf16[1,40,1152]{2,1,0:T(8,128)(2,1)S(1)}, u32[]{:S(2)}, u32[]{:S(2)}) collective-permute-start(bf16[1,40,1152]{2,1,0:T(8,128)(2,1)S(1)} %get-tuple-element.13), channel_id=1, source_target_pairs={{48,0},{0,16},{16,32},{32,48},{49,1},{1,17},{17,33},{33,49},{50,2}... | collective-permute-start | bytes 276488 | tf_op jit(solution)/shard_map/ppermute | solution.py:36
  25.9 11.6 %copy-start.3 = (bf16[224,896]{1,0:T(8,128)(2,1)S(1)}, bf16[224,896]{1,0:T(8,128)(2,1)}, u32[]{:S(2)}) copy-start(bf16[224,896]{1,0:T(8,128)(2,1)} %basis_own.1) | copy-start | bytes 1204228
  26.8 18.0 %all-to-all-start = ((bf16[8,2,80,224]{3,2,1,0:T(8,128)(2,1)}), bf16[8,2,80,224]{3,2,1,0:T(8,128)(2,1)S(1)}, u32[]{:S(2)}, u32[]{:S(2)}) async-start(bf16[8,2,80,224]{3,2,1,0:T(8,128)(2,1)} %both.1), calls=%async_computation | async-start | bytes 1310720 | tf_op jit(solution)/shard_map/all_to_all | solution.py:44
  35.0 16.5 %collective-permute-start.5 = (bf16[4,40,2304]{2,1,0:T(8,128)(2,1)S(1)}, bf16[4,40,2304]{2,1,0:T(8,128)(2,1)}, u32[]{:S(2)}, u32[]{:S(2)}) collective-permute-start(bf16[4,40,2304]{2,1,0:T(8,128)(2,1)S(1)} %along.1.earlier.refs_0_), channel_id=1, source_target_pairs={{64,0},{128,64},{192,128},{0,192},{65,1},{129,65},{193,129},{1,193... | collective-permute-start | bytes 2211848 | tf_op jit(solution)/shard_map/ppermute | solution.py:36
  37.5 17.3 %collective-permute-start.6 = (bf16[4,40,2304]{2,1,0:T(8,128)(2,1)S(1)}, bf16[4,40,2304]{2,1,0:T(8,128)(2,1)}, u32[]{:S(2)}, u32[]{:S(2)}) collective-permute-start(bf16[4,40,2304]{2,1,0:T(8,128)(2,1)S(1)} %along.1.earlier.refs_0_), channel_id=1, source_target_pairs={{192,0},{0,64},{64,128},{128,192},{193,1},{1,65},{65,129},{129,193... | collective-permute-start | bytes 2211848 | tf_op jit(solution)/shard_map/ppermute | solution.py:36
  37.5 3.4 %collective-permute-start.7 = (bf16[224,896]{1,0:T(8,128)(2,1)S(1)}, bf16[224,896]{1,0:T(8,128)(2,1)S(1)}, u32[]{:S(2)}, u32[]{:S(2)}) collective-permute-start(bf16[224,896]{1,0:T(8,128)(2,1)S(1)} %copy-done.3), channel_id=1, source_target_pairs={{8,0},{0,8},{9,1},{1,9},{10,2},{2,10},{11,3},{3,11},{12,4},{4,12},... | collective-permute-start | bytes 1204232 | tf_op jit(solution)/shard_map/ppermute | solution.py:36
  40.9 0.8 copy-start.4
  44.8 0.8 copy-start.1
  45.6 1.1 copy-start.2
  46.7 1.0 copy-start.5
  49.1 9.6 %copy-start = (bf16[2304,576]{0,1:T(8,128)(2,1)S(1)}, bf16[2304,576]{0,1:T(8,128)(2,1)}, u32[]{:S(2)}) copy-start(bf16[2304,576]{0,1:T(8,128)(2,1)} %param.11) | copy-start | bytes 7962628
  55.9 9.2 %collective-permute-start.10 = (bf16[4,40,1152]{2,1,0:T(8,128)(2,1)S(1)}, bf16[4,40,1152]{2,1,0:T(8,128)(2,1)S(1)}, u32[]{:S(2)}, u32[]{:S(2)}) collective-permute-start(bf16[4,40,1152]{2,1,0:T(8,128)(2,1)S(1)} %get-tuple-element.16), channel_id=1, source_target_pairs={{192,0},{0,64},{64,128},{128,192},{193,1},{1,65},{65,129},{129,193... | collective-permute-start | bytes 1105928 | tf_op jit(solution)/shard_map/ppermute | solution.py:36
  56.0 9.1 %collective-permute-start.9 = (bf16[4,40,1152]{2,1,0:T(8,128)(2,1)S(1)}, bf16[4,40,1152]{2,1,0:T(8,128)(2,1)S(1)}, u32[]{:S(2)}, u32[]{:S(2)}) collective-permute-start(bf16[4,40,1152]{2,1,0:T(8,128)(2,1)S(1)} %get-tuple-element.15.earlier), channel_id=1, source_target_pairs={{64,0},{128,64},{192,128},{0,192},{65,1},{129,65},{193,129},{1,193... | collective-permute-start | bytes 1105928 | tf_op jit(solution)/shard_map/ppermute | solution.py:36
  70.4 35.4 %all-to-all-start.1 = ((f16[8,72,1152]{2,1,0:T(8,128)(2,1)}), f16[8,72,1152]{2,1,0:T(8,128)(2,1)}, u32[]{:S(2)}, u32[]{:S(2)}) async-start(f16[8,72,1152]{2,1,0:T(8,128)(2,1)} %pad_maximum_fusion), calls=%async_computation.1 | async-start | bytes 2654208 | tf_op jit(solution)/shard_map/all_to_all | solution.py:44
  75.6 10.2 %collective-permute-start.12 = (f16[4,40,896]{2,1,0:T(8,128)(2,1)S(1)}, f16[4,40,896]{2,1,0:T(8,128)(2,1)S(1)}, u32[]{:S(2)}, u32[]{:S(2)}) collective-permute-start(f16[4,40,896]{2,1,0:T(8,128)(2,1)S(1)} %get-tuple-element.17), channel_id=1, source_target_pairs={{192,0},{0,64},{64,128},{128,192},{193,1},{1,65},{65,129},{129,193... | collective-permute-start | bytes 860168 | tf_op jit(solution)/shard_map/ppermute | solution.py:36
  75.7 10.3 %collective-permute-start.13 = (f16[4,40,896]{2,1,0:T(8,128)(2,1)S(1)}, f16[4,40,896]{2,1,0:T(8,128)(2,1)}, u32[]{:S(2)}, u32[]{:S(2)}) collective-permute-start(f16[4,40,896]{2,1,0:T(8,128)(2,1)S(1)} %get-tuple-element.19), channel_id=1, source_target_pairs={{128,0},{192,64},{0,128},{64,192},{129,1},{193,65},{1,129},{65,193... | collective-permute-start | bytes 860168 | tf_op jit(solution)/shard_map/ppermute | solution.py:36
  78.0 10.8 %collective-permute-start.14 = (f16[4,40,896]{2,1,0:T(8,128)(2,1)S(1)}, f16[4,40,896]{2,1,0:T(8,128)(2,1)}, u32[]{:S(2)}, u32[]{:S(2)}) collective-permute-start(f16[4,40,896]{2,1,0:T(8,128)(2,1)S(1)} %get-tuple-element.18), channel_id=1, source_target_pairs={{64,0},{128,64},{192,128},{0,192},{65,1},{129,65},{193,129},{1,193... | collective-permute-start | bytes 860168 | tf_op jit(solution)/shard_map/ppermute | solution.py:36
  90.1 5.4 %collective-permute-start.15 = (f16[40,896]{1,0:T(8,128)(2,1)S(1)}, f16[40,896]{1,0:T(8,128)(2,1)S(1)}, u32[]{:S(2)}, u32[]{:S(2)}) collective-permute-start(f16[40,896]{1,0:T(8,128)(2,1)S(1)} %get-tuple-element.20), channel_id=1, source_target_pairs={{48,0},{0,16},{16,32},{32,48},{49,1},{1,17},{17,33},{33,49},{50,2}... | collective-permute-start | bytes 215048 | tf_op jit(solution)/shard_map/ppermute | solution.py:36
  90.2 7.7 %collective-permute-start.16 = (f16[40,896]{1,0:T(8,128)(2,1)S(1)}, f16[40,896]{1,0:T(8,128)(2,1)S(1)}, u32[]{:S(2)}, u32[]{:S(2)}) collective-permute-start(f16[40,896]{1,0:T(8,128)(2,1)S(1)} %get-tuple-element.22), channel_id=1, source_target_pairs={{32,0},{48,16},{0,32},{16,48},{33,1},{49,17},{1,33},{17,49},{34,2}... | collective-permute-start | bytes 215048 | tf_op jit(solution)/shard_map/ppermute | solution.py:36
  94.7 4.3 %collective-permute-start.17 = (f16[40,896]{1,0:T(8,128)(2,1)S(1)}, f16[40,896]{1,0:T(8,128)(2,1)S(1)}, u32[]{:S(2)}, u32[]{:S(2)}) collective-permute-start(f16[40,896]{1,0:T(8,128)(2,1)S(1)} %get-tuple-element.21), channel_id=1, source_target_pairs={{16,0},{32,16},{48,32},{0,48},{17,1},{33,17},{49,33},{1,49},{18,2}... | collective-permute-start | bytes 215048 | tf_op jit(solution)/shard_map/ppermute | solution.py:36
  99.0 15.7 %collective-permute-start.18 = (bf16[40,896]{1,0:T(8,128)(2,1)S(1)}, bf16[40,896]{1,0:T(8,128)(2,1)S(1)}, u32[]{:S(2)}, u32[]{:S(2)}) collective-permute-start(bf16[40,896]{1,0:T(8,128)(2,1)S(1)} %fusion.7), channel_id=1, source_target_pairs={{16,0},{32,16},{48,32},{0,48},{17,1},{33,17},{49,33},{1,49},{18,2}... | collective-permute-start | bytes 215048 | tf_op jit(solution)/shard_map/ppermute | solution.py:36
  101.1 13.6 %collective-permute-start.19 = (bf16[40,896]{1,0:T(8,128)(2,1)S(1)}, bf16[40,896]{1,0:T(8,128)(2,1)S(1)}, u32[]{:S(2)}, u32[]{:S(2)}) collective-permute-start(bf16[40,896]{1,0:T(8,128)(2,1)S(1)} %fusion.7), channel_id=1, source_target_pairs={{32,0},{48,16},{0,32},{16,48},{33,1},{49,17},{1,33},{17,49},{34,2}... | collective-permute-start | bytes 215048 | tf_op jit(solution)/shard_map/ppermute | solution.py:36
  105.2 9.5 %collective-permute-start.20 = (bf16[40,896]{1,0:T(8,128)(2,1)S(1)}, bf16[40,896]{1,0:T(8,128)(2,1)S(1)}, u32[]{:S(2)}, u32[]{:S(2)}) collective-permute-start(bf16[40,896]{1,0:T(8,128)(2,1)S(1)} %fusion.7), channel_id=1, source_target_pairs={{48,0},{0,16},{16,32},{32,48},{49,1},{1,17},{17,33},{33,49},{50,2}... | collective-permute-start | bytes 215048 | tf_op jit(solution)/shard_map/ppermute | solution.py:36
  107.5 8.2 %collective-permute-start.11 = (bf16[72,576]{1,0:T(8,128)(2,1)S(1)}, bf16[72,576]{1,0:T(8,128)(2,1)S(1)}, u32[]{:S(2)}, u32[]{:S(2)}) collective-permute-start(bf16[72,576]{1,0:T(8,128)(2,1)S(1)} %get-tuple-element.23), channel_id=1, source_target_pairs={{8,0},{0,8},{9,1},{1,9},{10,2},{2,10},{11,3},{3,11},{12,4},{4,12},... | collective-permute-start | bytes 248840 | tf_op jit(solution)/shard_map/ppermute | solution.py:36
  117.4 24.3 %all-to-all-start.2 = ((bf16[8,2,72,576]{3,2,1,0:T(8,128)(2,1)}), bf16[8,2,72,576]{3,2,1,0:T(8,128)(2,1)S(1)}, u32[]{:S(2)}, u32[]{:S(2)}) async-start(bf16[8,2,72,576]{3,2,1,0:T(8,128)(2,1)} %shares.1), calls=%async_computation.2 | async-start | bytes 2949120 | tf_op jit(solution)/shard_map/all_to_all | solution.py:44
  122.1 7.5 %collective-permute-start.21 = (bf16[4,40,896]{2,1,0:T(8,128)(2,1)S(1)}, bf16[4,40,896]{2,1,0:T(8,128)(2,1)S(1)}, u32[]{:S(2)}, u32[]{:S(2)}) collective-permute-start(bf16[4,40,896]{2,1,0:T(8,128)(2,1)S(1)} %pad_maximum_fusion.1.earlier.refs_0_), channel_id=1, source_target_pairs={{64,0},{128,64},{192,128},{0,192},{65,1},{129,65},{193,129},{1,193... | collective-permute-start | bytes 860168 | tf_op jit(solution)/shard_map/ppermute | solution.py:36
  122.7 14.2 %collective-permute-start.22 = (bf16[4,40,896]{2,1,0:T(8,128)(2,1)S(1)}, bf16[4,40,896]{2,1,0:T(8,128)(2,1)S(1)}, u32[]{:S(2)}, u32[]{:S(2)}) collective-permute-start(bf16[4,40,896]{2,1,0:T(8,128)(2,1)S(1)} %pad_maximum_fusion.1.earlier.refs_0_), channel_id=1, source_target_pairs={{128,0},{192,64},{0,128},{64,192},{129,1},{193,65},{1,129},{65,193... | collective-permute-start | bytes 860168 | tf_op jit(solution)/shard_map/ppermute | solution.py:36
  122.8 14.1 %collective-permute-start.23 = (bf16[4,40,896]{2,1,0:T(8,128)(2,1)S(1)}, bf16[4,40,896]{2,1,0:T(8,128)(2,1)S(1)}, u32[]{:S(2)}, u32[]{:S(2)}) collective-permute-start(bf16[4,40,896]{2,1,0:T(8,128)(2,1)S(1)} %pad_maximum_fusion.1.earlier.refs_0_), channel_id=1, source_target_pairs={{192,0},{0,64},{64,128},{128,192},{193,1},{1,65},{65,129},{129,193... | collective-permute-start | bytes 860168 | tf_op jit(solution)/shard_map/ppermute | solution.py:36
  123.5 16.9 %collective-permute-start.24 = (bf16[4,40,896]{2,1,0:T(8,128)(2,1)S(1)}, bf16[4,40,896]{2,1,0:T(8,128)(2,1)S(1)}, u32[]{:S(2)}, u32[]{:S(2)}) collective-permute-start(bf16[4,40,896]{2,1,0:T(8,128)(2,1)S(1)} %pad_maximum_fusion.1.earlier.refs_0_), channel_id=1, source_target_pairs={{8,0},{0,8},{9,1},{1,9},{10,2},{2,10},{11,3},{3,11},{12,4},{4,12},... | collective-permute-start | bytes 860168 | tf_op jit(solution)/shard_map/ppermute | solution.py:36
  129.5 10.9 %collective-permute-start.25 = (bf16[4,40,896]{2,1,0:T(8,128)(2,1)S(1)}, bf16[4,40,896]{2,1,0:T(8,128)(2,1)S(1)}, u32[]{:S(2)}, u32[]{:S(2)}) collective-permute-start(bf16[4,40,896]{2,1,0:T(8,128)(2,1)S(1)} %collective-permute-done.21.refs_1_), channel_id=1, source_target_pairs={{8,0},{0,8},{9,1},{1,9},{10,2},{2,10},{11,3},{3,11},{12,4},{4,12},... | collective-permute-start | bytes 860168 | tf_op jit(solution)/shard_map/ppermute | solution.py:36
  136.9 3.6 %collective-permute-start.26 = (bf16[4,40,896]{2,1,0:T(8,128)(2,1)S(1)}, bf16[4,40,896]{2,1,0:T(8,128)(2,1)S(1)}, u32[]{:S(2)}, u32[]{:S(2)}) collective-permute-start(bf16[4,40,896]{2,1,0:T(8,128)(2,1)S(1)} %collective-permute-done.22.refs_2_), channel_id=1, source_target_pairs={{8,0},{0,8},{9,1},{1,9},{10,2},{2,10},{11,3},{3,11},{12,4},{4,12},... | collective-permute-start | bytes 860168 | tf_op jit(solution)/shard_map/ppermute | solution.py:36
  136.9 4.1 %collective-permute-start.27 = (bf16[4,40,896]{2,1,0:T(8,128)(2,1)S(1)}, bf16[4,40,896]{2,1,0:T(8,128)(2,1)S(1)}, u32[]{:S(2)}, u32[]{:S(2)}) collective-permute-start(bf16[4,40,896]{2,1,0:T(8,128)(2,1)S(1)} %collective-permute-done.23.refs_3_), channel_id=1, source_target_pairs={{8,0},{0,8},{9,1},{1,9},{10,2},{2,10},{11,3},{3,11},{12,4},{4,12},... | collective-permute-start | bytes 860168 | tf_op jit(solution)/shard_map/ppermute | solution.py:36
  141.0 0.7 copy-start.6
  141.7 1.0 copy-start.7
